TPU v7x, 128 devices: a whole 4x4x4 slice. The times are simulated.
128 devices in a mesh: row: 8 (over y, x_hi), col: 16 (over x_lo, z, core).
Axes of the slice: x: 4 (x_hi: 2, x_lo: 2; x = x_hi * 2 + x_lo), y: 4, z: 4, core: 2. Of those that a mesh axis runs over, the one named last changes fastest.
Arguments:
- tokens: bfloat16 [1024, 6144], P('row', 'col'), may hold values from -6 to 6
- cotangent: bfloat16 [1024, 6144], P('row', 'col'), may hold values from -6 to 6
- w_in: bfloat16 [6144, 24576], P('col', 'row'), may hold values from -0.078125 to 0.078125
- w_out: bfloat16 [24576, 6144], P('row', 'col'), may hold values from -0.0390625 to 0.0390625
Outputs:
- input_grad: bfloat16 [1024, 6144], P('row', 'col')
- w_in_grad: bfloat16 [6144, 24576], P('col', 'row')
- w_out_grad: bfloat16 [24576, 6144], P('row', 'col')
All inputs are finite; a program needn't handle non-finite values.
Results may differ from a plain program's by a relative error of at most 0.0049.
Values may be sent and summed in bfloat16 or wider, within the bound.
No kernel may reach another device: no remote copies, remote signals or barrier semaphores. Data moves between devices by JAX's collectives and lax.ppermute only.
A program may use at most 128 MiB of HBM per device.

v0:
```python
import jax
import jax.numpy as jnp
from jax import lax
from jax.sharding import Mesh
from jax.sharding import PartitionSpec as P

AXES = ("y", "xh", "xl", "z", "core")
SIZES = (4, 2, 2, 4, 2)
ROWS = ("y", "xh")
COLS = ("xl", "z", "core")
F32 = jnp.float32
BF16 = jnp.bfloat16


def gelu_parts(pre):
    cdf = 0.5 * (1.0 + lax.erf(pre * 0.7071067811865476))
    pdf = jnp.exp(-0.5 * pre * pre) * 0.3989422804014327
    return (cdf, pdf)


def shift(x, axis, by):
    n = SIZES[AXES.index(axis)]
    return lax.ppermute(x, axis, [(i, (i + by) % n) for i in range(n)])


def dot(a, b, da, db):
    return lax.dot_general(a, b, (((da,), (db,)), ((), ())), preferred_element_type=F32)


def swap_halves(first, second, flag, axis):
    return jnp.concatenate([jnp.where(flag == 0, first, second), jnp.where(flag == 0, second, first)], axis)


def gate(value, *after):
    return lax.optimization_barrier((value, after))[0]


def local(tokens, cotangent, w_in, w_out):
    z, core = lax.axis_index("z"), lax.axis_index("core")
    rows, feat = tokens.shape
    hid = w_in.shape[1] // 2
    piece = rows // 4

    def relative(a, sign):
        return jnp.roll(a.reshape(4, piece, a.shape[-1]), sign * z, 0)

    def halves(w, axis):
        keep = lax.dynamic_slice_in_dim(w, core * hid, hid, axis)
        return keep, lax.dynamic_slice_in_dim(w, (1 - core) * hid, hid, axis)

    def features(a, b):
        return (
            jnp.concatenate([a[..., :feat], b[..., :feat]], -1),
            jnp.concatenate([a[..., feat:], b[..., feat:]], -1),
        )

    def cat(p, g):
        return jnp.concatenate([p.astype(BF16), g.astype(BF16)], 1)

    def up_down(up, down):
        return shift(up, "z", 1), shift(down, "z", -1)

    def step1(tok, cot):
        return dot(tok[2], wi, 1, 0).astype(BF16), dot(cot[2], wo, 1, 1).astype(BF16)

    def step2(tok, cot, up, down):
        return (
            cat(dot(tok[1], wi, 1, 0) + up.astype(F32), dot(cot[1], wo, 1, 1)),
            cat(dot(tok[3], wi, 1, 0), dot(cot[3], wo, 1, 1) + down.astype(F32)),
        )

    def step3(tok, cot, up, down):
        p = dot(tok[0], wi, 1, 0) + up[:, :hid].astype(F32) + down[:, :hid].astype(F32)
        g = dot(cot[0], wo, 1, 1) + up[:, hid:].astype(F32) + down[:, hid:].astype(F32)
        return p, g, cat(p, g)

    def step4(p, g, other):
        p = p + other[:, :hid].astype(F32)
        g = g + other[:, hid:].astype(F32)
        cdf, pdf = gelu_parts(p)
        return cat(p * cdf, g * (cdf + p * pdf))

    def send_mine(mine):
        return shift(mine, "z", -1), shift(mine, "z", 1)

    def send_on(above, below):
        return shift(above[:, :hid], "z", -1), shift(below[:, hid:], "z", 1)

    def gathered(mine, above, below, act2, grad2):
        act = jnp.concatenate([mine[:, :hid], above[:, :hid], act2, below[:, :hid]], 0)
        grad = jnp.concatenate([mine[:, hid:], above[:, hid:], grad2, below[:, hid:]], 0)
        return act, grad

    def input_part(grad):
        part = dot(grad, wi, 1, 1)
        return part[:, :feat], part[:, feat:]

    def by_row(mine, other):
        return (mine + other).reshape(4, -1, piece, feat)

    own = relative(jnp.concatenate([tokens, cotangent], 1), -1)
    near = [own] + [shift(own, "y", -d) for d in (1, 2, 3)]
    wi_keep, wi_send = halves(w_in, 1)
    wo_keep, wo_send = halves(w_out, 0)
    wi_got, wo_got = shift(wi_send, "core", 1), shift(wo_send, "core", 1)
    across = shift(own, "xh", 1)
    near = jnp.concatenate(near, 1)
    near_other = shift(near, "core", 1)
    wi = jnp.concatenate([wi_keep, wi_got], 0)
    wo = jnp.concatenate([wo_keep, wo_got], 1)
    wi, wo = lax.optimization_barrier((wi, wo))

    tok_a, cot_a = features(near, near_other)
    m_a = step1(tok_a, cot_a)
    r_a = up_down(*m_a)

    across = gate(across, m_a)
    far = [across] + [shift(across, "y", -d) for d in (1, 2, 3)]

    m_a = step2(tok_a, cot_a, *gate(r_a, across))
    r_a = up_down(*m_a)

    far = jnp.concatenate(gate(far, m_a), 1)
    far_other = shift(far, "core", 1)
    tok_b, cot_b = features(far, far_other)
    m_b = step1(tok_b, cot_b)
    r_b = up_down(*m_b)

    p_a, g_a, m_a = step3(tok_a, cot_a, *gate(r_a, m_b))
    x_a = shift(m_a, "xl", 1)

    m_b = step2(tok_b, cot_b, *gate(r_b, m_a))
    r_b = up_down(*m_b)

    mine_a = step4(p_a, g_a, gate(x_a, m_b))
    s_a = send_mine(mine_a)

    p_b, g_b, m_b = step3(tok_b, cot_b, *gate(r_b, mine_a))
    x_b = shift(m_b, "xl", 1)

    s_a = gate(s_a, m_b)
    t_a = send_on(*s_a)

    mine_b = step4(p_b, g_b, gate(x_b, s_a))
    s_b = send_mine(mine_b)

    act_a, grad_a = gathered(mine_a, *s_a, *gate(t_a, mine_b))
    in_a, in_a_other = input_part(grad_a)
    in_a_got = shift(in_a_other, "core", 1)

    s_b = gate(s_b, in_a_other)
    t_b = send_on(*s_b)

    back_a = by_row(in_a, gate(in_a_got, s_b))
    back = [shift(back_a[:, d].astype(BF16), "y", d) for d in (1, 2, 3)]

    act_b, grad_b = gathered(mine_b, *s_b, *gate(t_b, back_a))
    in_b, in_b_other = input_part(grad_b)
    in_b_got = shift(in_b_other, "core", 1)
    back_b = by_row(in_b, in_b_got).astype(BF16)
    back += [
        lax.ppermute(back_b[:, d], ROWS, [(i, ((i // 2 + d) % 4) * 2 + (i + 1) % 2) for i in range(8)])
        for d in (0, 1, 2, 3)
    ]

    def token_sum(left, right):
        return (dot(left[0], right[0], 0, 0) + dot(left[1], right[1], 0, 0)).astype(BF16)

    flat = lambda a: a.reshape(-1, a.shape[-1])
    toks = [flat(a) for a in (tok_a, tok_b)]
    cots = [flat(a) for a in (cot_a, cot_b)]
    grads, acts = [grad_a, grad_b], [act_a, act_b]
    wi_other = shift(token_sum([t[:, feat:] for t in toks], grads), "core", 1)
    wo_other = shift(token_sum(acts, [c[:, feat:] for c in cots]), "core", 1)
    wi_own = token_sum([t[:, :feat] for t in toks], grads)
    wo_own = token_sum(acts, [c[:, :feat] for c in cots])
    w_in_grad = swap_halves(wi_own, wi_other, core, 1)
    w_out_grad = swap_halves(wo_own, wo_other, core, 0)

    total = back_a[:, 0]
    for part in back:
        total = total + part.astype(F32)
    input_grad = relative(total, 1).reshape(rows, feat).astype(BF16)
    return (input_grad, w_in_grad, w_out_grad)


def solution(mesh):
    fine = Mesh(mesh.devices.reshape(SIZES), AXES)
    return jax.shard_map(
        local,
        mesh=fine,
        in_specs=(P(ROWS, COLS), P(ROWS, COLS), P(COLS, ROWS), P(ROWS, COLS)),
        out_specs=(P(ROWS, COLS), P(COLS, ROWS), P(ROWS, COLS)),
        check_vma=False,
    )
```

profile of v0, /device:TPU:0, one launch (start us, length us, event | category | flops | bytes accessed | tf_op | source)
XLA Modules:
  0.0 185.4 jit_solution(4351804539208079657)
XLA Ops:
  0.7 1.0 pad_maximum_fusion.25
  2.4 1.7 collective-permute-start.2
  4.0 2.9 %collective-permute-start.1 = (bf16[4,32,768]{2,1,0:T(8,128)(2,1)}, bf16[4,32,768]{2,1,0:T(8,128)(2,1)S(1)}, u32[]{:S(2)}, u32[]{:S(2)}) collective-permute-start(bf16[4,32,768]{2,1,0:T(8,128)(2,1)} %fusion.35), channel_id=1, source_target_pairs={{0,64},{32,96},{64,0},{96,32},{1,65},{33,97},{65,1},{97,33},{2,66}... | collective-permute-start | bytes 589832 | tf_op jit(solution)/shard_map/ppermute | solution.py:23
  6.9 1.3 collective-permute-start
  8.3 1.9 %constant_dynamic-slice_fusion.3 = (bf16[384,1536]{1,0:T(8,128)(2,1)S(1)}, bf16[384,1536]{1,0:T(8,128)(2,1)S(1)}) fusion(bf16[384,3072]{1,0:T(8,128)(2,1)} %param.6, s32[]{:T(128)S(6)} %select_n.57, s32[]{:T(128)S(6)} %select_n.58), kind=kLoop, calls=%fused_computation.190 | loop fusion | bytes 4718600 | tf_op jit(solution)/shard_map/dynamic_slice | solution.py:48
  10.6 5.4 %collective-permute-done.1 = bf16[4,32,768]{2,1,0:T(8,128)(2,1)S(1)} collective-permute-done((bf16[4,32,768]{2,1,0:T(8,128)(2,1)}, bf16[4,32,768]{2,1,0:T(8,128)(2,1)S(1)}, u32[]{:S(2)}, u32[]{:S(2)}) %collective-permute-start.1) | collective-permute-done | bytes 196640 | tf_op jit(solution)/shard_map/ppermute | solution.py:23
  16.0 1.0 pad_maximum_fusion.12
  17.9 3.0 %collective-permute-start.8 = (bf16[4,32,768]{2,1,0:T(8,128)(2,1)}, bf16[4,32,768]{2,1,0:T(8,128)(2,1)S(1)}, u32[]{:S(2)}, u32[]{:S(2)}) collective-permute-start(bf16[4,32,768]{2,1,0:T(8,128)(2,1)} %fusion.35), channel_id=1, source_target_pairs={{0,16},{16,0},{1,17},{17,1},{2,18},{18,2},{3,19},{19,3},{4,20},{20... | collective-permute-start | bytes 589832 | tf_op jit(solution)/shard_map/ppermute | solution.py:23
  22.0 2.0 %collective-permute-start.6 = (bf16[128,1536]{1,0:T(8,128)(2,1)S(1)}, bf16[128,1536]{1,0:T(8,128)(2,1)S(1)}, u32[]{:S(2)}, u32[]{:S(2)}) collective-permute-start(bf16[128,1536]{1,0:T(8,128)(2,1)S(1)} %convolution_convert_fusion.7), channel_id=1, source_target_pairs={{0,2},{2,4},{4,6},{6,0},{1,3},{3,5},{5,7},{7,1},{8,10},{10,12},{12... | collective-permute-start | bytes 1179656 | tf_op jit(solution)/shard_map/ppermute | solution.py:23
  24.0 0.9 convolution_convert_fusion.6
  24.9 2.2 %collective-permute-start.7 = (bf16[128,1536]{1,0:T(8,128)(2,1)S(1)}, bf16[128,1536]{1,0:T(8,128)(2,1)S(1)}, u32[]{:S(2)}, u32[]{:S(2)}) collective-permute-start(bf16[128,1536]{1,0:T(8,128)(2,1)S(1)} %convolution_convert_fusion.6), channel_id=1, source_target_pairs={{0,6},{2,0},{4,2},{6,4},{1,7},{3,1},{5,3},{7,5},{8,14},{10,8},{12,... | collective-permute-start | bytes 1179656 | tf_op jit(solution)/shard_map/ppermute | solution.py:23
  27.1 0.9 convolution_convert_fusion.5
  28.0 2.1 %collective-permute-start.11 = (bf16[4,32,768]{2,1,0:T(8,128)(2,1)S(1)}, bf16[4,32,768]{2,1,0:T(8,128)(2,1)S(1)}, u32[]{:S(2)}, u32[]{:S(2)}) collective-permute-start(bf16[4,32,768]{2,1,0:T(8,128)(2,1)S(1)} %collective-permute-done.8), channel_id=1, source_target_pairs={{0,96},{32,0},{64,32},{96,64},{1,97},{33,1},{65,33},{97,65},{2,98}... | collective-permute-start | bytes 589832 | tf_op jit(solution)/shard_map/ppermute | solution.py:23
  30.1 1.1 collective-permute-start.12
  32.5 2.7 %collective-permute-done.6 = bf16[128,1536]{1,0:T(8,128)(2,1)S(1)} collective-permute-done((bf16[128,1536]{1,0:T(8,128)(2,1)S(1)}, bf16[128,1536]{1,0:T(8,128)(2,1)S(1)}, u32[]{:S(2)}, u32[]{:S(2)}) %collective-permute-start.6) | collective-permute-done | bytes 393248 | tf_op jit(solution)/shard_map/ppermute | solution.py:23
  36.2 0.9 add_convert_fusion.2
  37.1 1.0 pad_maximum_fusion.13
  38.1 1.0 pad_maximum_fusion.14
  39.5 2.4 %collective-permute-done.13 = bf16[4,32,768]{2,1,0:T(8,128)(2,1)S(1)} collective-permute-done((bf16[4,32,768]{2,1,0:T(8,128)(2,1)S(1)}, bf16[4,32,768]{2,1,0:T(8,128)(2,1)S(1)}, u32[]{:S(2)}, u32[]{:S(2)}) %collective-permute-start.13) | collective-permute-done | bytes 196640 | tf_op jit(solution)/shard_map/ppermute | solution.py:23
  44.8 1.3 pad_maximum_fusion.8
  46.6 0.9 fusion.86
  47.9 3.0 %collective-permute-start.10 = (bf16[128,3072]{1,0:T(8,128)(2,1)S(1)}, bf16[128,3072]{1,0:T(8,128)(2,1)S(1)}, u32[]{:S(2)}, u32[]{:S(2)}) collective-permute-start(bf16[128,3072]{1,0:T(8,128)(2,1)S(1)} %copy-done.5), channel_id=1, source_target_pairs={{0,6},{2,0},{4,2},{6,4},{1,7},{3,1},{5,3},{7,5},{8,14},{10,8},{12,... | collective-permute-start | bytes 2359304 | tf_op jit(solution)/shard_map/ppermute | solution.py:23
  51.0 1.2 fusion.134
  52.2 1.2 fusion.133
  53.9 0.9 convolution_convert_fusion.2
  54.8 3.5 %collective-permute-start.17 = (bf16[128,1536]{1,0:T(8,128)(2,1)S(1)}, bf16[128,1536]{1,0:T(8,128)(2,1)S(1)}, u32[]{:S(2)}, u32[]{:S(2)}) collective-permute-start(bf16[128,1536]{1,0:T(8,128)(2,1)S(1)} %convolution_convert_fusion.2), channel_id=1, source_target_pairs={{0,6},{2,0},{4,2},{6,4},{1,7},{3,1},{5,3},{7,5},{8,14},{10,8},{12,... | collective-permute-start | bytes 1179656 | tf_op jit(solution)/shard_map/ppermute | solution.py:23
  58.3 0.9 convolution_convert_fusion.1
  59.2 10.1 %collective-permute-done.9 = bf16[128,3072]{1,0:T(8,128)(2,1)S(1)} collective-permute-done((bf16[128,3072]{1,0:T(8,128)(2,1)S(1)}, bf16[128,3072]{1,0:T(8,128)(2,1)S(1)}, u32[]{:S(2)}, u32[]{:S(2)}) %collective-permute-start.9) | collective-permute-done | bytes 786464 | tf_op jit(solution)/shard_map/ppermute | solution.py:23
  70.4 1.6 collective-permute-start.15
  72.0 0.9 fusion.50
  72.9 4.4 %collective-permute-done.16 = bf16[128,1536]{1,0:T(8,128)(2,1)S(1)} collective-permute-done((bf16[128,1536]{1,0:T(8,128)(2,1)S(1)}, bf16[128,1536]{1,0:T(8,128)(2,1)S(1)}, u32[]{:S(2)}, u32[]{:S(2)}) %collective-permute-start.16) | collective-permute-done | bytes 393248 | tf_op jit(solution)/shard_map/ppermute | solution.py:23
  78.4 0.9 add_convert_fusion
  79.4 2.8 %collective-permute-start.21 = (bf16[128,3072]{1,0:T(8,128)(2,1)S(1)}, bf16[128,3072]{1,0:T(8,128)(2,1)S(1)}, u32[]{:S(2)}, u32[]{:S(2)}) collective-permute-start(bf16[128,3072]{1,0:T(8,128)(2,1)S(1)} %pad_maximum_fusion.17), channel_id=1, source_target_pairs={{0,6},{2,0},{4,2},{6,4},{1,7},{3,1},{5,3},{7,5},{8,14},{10,8},{12,... | collective-permute-start | bytes 2359304 | tf_op jit(solution)/shard_map/ppermute | solution.py:23
  82.2 7.0 %collective-permute-done.15 = bf16[128,3072]{1,0:T(8,128)(2,1)S(1)} collective-permute-done((bf16[128,3072]{1,0:T(8,128)(2,1)S(1)}, bf16[128,3072]{1,0:T(8,128)(2,1)S(1)}, u32[]{:S(2)}, u32[]{:S(2)}) %collective-permute-start.15) | collective-permute-done | bytes 786464 | tf_op jit(solution)/shard_map/ppermute | solution.py:23
  90.0 2.7 %collective-permute-start.18 = (bf16[128,3072]{1,0:T(8,128)(2,1)S(1)}, bf16[128,3072]{1,0:T(8,128)(2,1)S(1)}, u32[]{:S(2)}, u32[]{:S(2)}) collective-permute-start(bf16[128,3072]{1,0:T(8,128)(2,1)S(1)} %pad_maximum_fusion.18), channel_id=1, source_target_pairs={{0,6},{2,0},{4,2},{6,4},{1,7},{3,1},{5,3},{7,5},{8,14},{10,8},{12,... | collective-permute-start | bytes 2359304 | tf_op jit(solution)/shard_map/ppermute | solution.py:23
  92.9 6.7 %collective-permute-done.20 = bf16[128,3072]{1,0:T(8,128)(2,1)S(1)} collective-permute-done((bf16[128,3072]{1,0:T(8,128)(2,1)S(1)}, bf16[128,3072]{1,0:T(8,128)(2,1)S(1)}, u32[]{:S(2)}, u32[]{:S(2)}) %collective-permute-start.20) | collective-permute-done | bytes 786464 | tf_op jit(solution)/shard_map/ppermute | solution.py:23
  100.9 1.6 collective-permute-start.24
  102.4 13.0 %collective-permute-done.18 = bf16[128,3072]{1,0:T(8,128)(2,1)S(1)} collective-permute-done((bf16[128,3072]{1,0:T(8,128)(2,1)S(1)}, bf16[128,3072]{1,0:T(8,128)(2,1)S(1)}, u32[]{:S(2)}, u32[]{:S(2)}) %collective-permute-start.18) | collective-permute-done | bytes 786464 | tf_op jit(solution)/shard_map/ppermute | solution.py:23
  115.5 3.8 %collective-permute-start.22 = (bf16[128,1536]{1,0:T(8,128)(2,1)S(1)}, bf16[128,1536]{1,0:T(8,128)(2,1)S(1)}, u32[]{:S(2)}, u32[]{:S(2)}) collective-permute-start(bf16[128,1536]{1,0:T(8,128)(2,1)S(1)} %get-tuple-element.78), channel_id=1, source_target_pairs={{0,6},{2,0},{4,2},{6,4},{1,7},{3,1},{5,3},{7,5},{8,14},{10,8},{12,... | collective-permute-start | bytes 1179656 | tf_op jit(solution)/shard_map/ppermute | solution.py:23
  120.2 3.3 %collective-permute-start.26 = (bf16[128,3072]{1,0:T(8,128)(2,1)S(1)}, bf16[128,3072]{1,0:T(8,128)(2,1)S(1)}, u32[]{:S(2)}, u32[]{:S(2)}) collective-permute-start(bf16[128,3072]{1,0:T(8,128)(2,1)S(1)} %pad_maximum_fusion.20), channel_id=1, source_target_pairs={{0,6},{2,0},{4,2},{6,4},{1,7},{3,1},{5,3},{7,5},{8,14},{10,8},{12,... | collective-permute-start | bytes 2359304 | tf_op jit(solution)/shard_map/ppermute | solution.py:23
  123.5 5.4 %collective-permute-done.22 = bf16[128,1536]{1,0:T(8,128)(2,1)S(1)} collective-permute-done((bf16[128,1536]{1,0:T(8,128)(2,1)S(1)}, bf16[128,1536]{1,0:T(8,128)(2,1)S(1)}, u32[]{:S(2)}, u32[]{:S(2)}) %collective-permute-start.22) | collective-permute-done | bytes 393248 | tf_op jit(solution)/shard_map/ppermute | solution.py:23
  128.9 3.8 %collective-permute-done.23 = bf16[128,1536]{1,0:T(8,128)(2,1)S(1)} collective-permute-done((bf16[128,1536]{1,0:T(8,128)(2,1)S(1)}, bf16[128,1536]{1,0:T(8,128)(2,1)S(1)}, u32[]{:S(2)}, u32[]{:S(2)}) %collective-permute-start.23) | collective-permute-done | bytes 393248 | tf_op jit(solution)/shard_map/ppermute | solution.py:23
  132.7 1.4 fusion.128
  134.3 1.0 fusion.18
  135.3 1.0 fusion.21
  136.3 6.9 %collective-permute-done.26 = bf16[128,3072]{1,0:T(8,128)(2,1)S(1)} collective-permute-done((bf16[128,3072]{1,0:T(8,128)(2,1)S(1)}, bf16[128,3072]{1,0:T(8,128)(2,1)S(1)}, u32[]{:S(2)}, u32[]{:S(2)}) %collective-permute-start.26) | collective-permute-done | bytes 786464 | tf_op jit(solution)/shard_map/ppermute | solution.py:23
  143.2 3.5 %collective-permute-done.27 = bf16[128,3072]{1,0:T(8,128)(2,1)S(1)} collective-permute-done((bf16[128,3072]{1,0:T(8,128)(2,1)S(1)}, bf16[128,3072]{1,0:T(8,128)(2,1)S(1)}, u32[]{:S(2)}, u32[]{:S(2)}) %collective-permute-start.27) | collective-permute-done | bytes 786464 | tf_op jit(solution)/shard_map/ppermute | solution.py:23
  147.1 2.2 %collective-permute-start.32 = (bf16[128,1536]{1,0:T(8,128)(2,1)S(1)}, bf16[128,1536]{1,0:T(8,128)(2,1)S(1)}, u32[]{:S(2)}, u32[]{:S(2)}) collective-permute-start(bf16[128,1536]{1,0:T(8,128)(2,1)S(1)} %get-tuple-element.72), channel_id=1, source_target_pairs={{0,2},{2,4},{4,6},{6,0},{1,3},{3,5},{5,7},{7,1},{8,10},{10,12},{12... | collective-permute-start | bytes 1179656 | tf_op jit(solution)/shard_map/ppermute | solution.py:23
  149.2 0.8 fusion.24
  150.2 5.1 %collective-permute-done.31 = bf16[128,1536]{1,0:T(8,128)(2,1)S(1)} collective-permute-done((bf16[128,1536]{1,0:T(8,128)(2,1)S(1)}, bf16[128,1536]{1,0:T(8,128)(2,1)S(1)}, u32[]{:S(2)}, u32[]{:S(2)}) %collective-permute-start.31) | collective-permute-done | bytes 393248 | tf_op jit(solution)/shard_map/ppermute | solution.py:23
  155.2 1.7 collective-permute-done.32
  156.9 1.4 fusion.127
  158.5 0.8 fusion.27
  160.1 1.2 collective-permute-start.29
  162.0 0.8 fusion.1
  163.1 5.0 %collective-permute-start.37 = (bf16[4,32,384]{2,1,0:T(8,128)(2,1)S(1)}, bf16[4,32,384]{2,1,0:T(8,128)(2,1)S(1)}, u32[]{:S(2)}, u32[]{:S(2)}) collective-permute-start(bf16[4,32,384]{2,1,0:T(8,128)(2,1)S(1)} %get-tuple-element.93), channel_id=1, source_target_pairs={{0,112},{16,96},{32,16},{48,0},{64,48},{80,32},{96,80},{112,64},{1... | collective-permute-start | bytes 294920 | tf_op jit(solution)/shard_map/ppermute | solution.py:162
  168.1 1.2 collective-permute-start.36
  169.3 3.7 %collective-permute-start.35 = (bf16[4,32,384]{2,1,0:T(8,128)(2,1)S(1)}, bf16[4,32,384]{2,1,0:T(8,128)(2,1)S(1)}, u32[]{:S(2)}, u32[]{:S(2)}) collective-permute-start(bf16[4,32,384]{2,1,0:T(8,128)(2,1)S(1)} %get-tuple-element.92), channel_id=1, source_target_pairs={{0,48},{16,32},{32,80},{48,64},{64,112},{80,96},{96,16},{112,0},{1... | collective-permute-start | bytes 294920 | tf_op jit(solution)/shard_map/ppermute | solution.py:162
  173.6 1.0 fusion.3
  174.7 4.1 %collective-permute-done.36 = bf16[4,32,384]{2,1,0:T(8,128)(2,1)S(1)} collective-permute-done((bf16[4,32,384]{2,1,0:T(8,128)(2,1)S(1)}, bf16[4,32,384]{2,1,0:T(8,128)(2,1)S(1)}, u32[]{:S(2)}, u32[]{:S(2)}) %collective-permute-start.36) | collective-permute-done | bytes 98336 | tf_op jit(solution)/shard_map/ppermute | solution.py:162
  180.1 0.8 broadcast_select_fusion.3
  180.9 1.7 pad_maximum_fusion.2
  182.7 1.1 broadcast_select_fusion.1
  183.7 1.6 pad_maximum_fusion.3
  (98 shorter events, 19.8 us)
Async XLA Ops:
  2.4 8.2 %collective-permute-start.2 = (bf16[4,32,768]{2,1,0:T(8,128)(2,1)}, bf16[4,32,768]{2,1,0:T(8,128)(2,1)S(1)}, u32[]{:S(2)}, u32[]{:S(2)}) collective-permute-start(bf16[4,32,768]{2,1,0:T(8,128)(2,1)} %fusion.35), channel_id=1, source_target_pairs={{0,32},{32,64},{64,96},{96,0},{1,33},{33,65},{65,97},{97,1},{2,34}... | collective-permute-start | bytes 589832 | tf_op jit(solution)/shard_map/ppermute | solution.py:23
  4.0 11.9 %collective-permute-start.1 = (bf16[4,32,768]{2,1,0:T(8,128)(2,1)}, bf16[4,32,768]{2,1,0:T(8,128)(2,1)S(1)}, u32[]{:S(2)}, u32[]{:S(2)}) collective-permute-start(bf16[4,32,768]{2,1,0:T(8,128)(2,1)} %fusion.35), channel_id=1, source_target_pairs={{0,64},{32,96},{64,0},{96,32},{1,65},{33,97},{65,1},{97,33},{2,66}... | collective-permute-start | bytes 589832 | tf_op jit(solution)/shard_map/ppermute | solution.py:23
  6.9 9.0 %collective-permute-start = (bf16[4,32,768]{2,1,0:T(8,128)(2,1)}, bf16[4,32,768]{2,1,0:T(8,128)(2,1)S(1)}, u32[]{:S(2)}, u32[]{:S(2)}) collective-permute-start(bf16[4,32,768]{2,1,0:T(8,128)(2,1)} %fusion.35), channel_id=1, source_target_pairs={{0,96},{32,0},{64,32},{96,64},{1,97},{33,1},{65,33},{97,65},{2,98}... | collective-permute-start | bytes 589832 | tf_op jit(solution)/shard_map/ppermute | solution.py:23
  8.3 8.8 %copy-start.4 = (bf16[3072,384]{1,0:T(8,128)(2,1)S(1)}, bf16[3072,384]{1,0:T(8,128)(2,1)}, u32[]{:S(2)}) copy-start(bf16[3072,384]{1,0:T(8,128)(2,1)} %param.7) | copy-start | bytes 7077892
  10.2 10.9 %collective-permute-start.4 = (bf16[384,1536]{1,0:T(8,128)(2,1)S(1)}, bf16[384,1536]{1,0:T(8,128)(2,1)S(1)}, u32[]{:S(2)}, u32[]{:S(2)}) collective-permute-start(bf16[384,1536]{1,0:T(8,128)(2,1)S(1)} %get-tuple-element.66), channel_id=1, source_target_pairs={{0,1},{1,0},{2,3},{3,2},{4,5},{5,4},{6,7},{7,6},{8,9},{9,8},{10,11... | collective-permute-start | bytes 3538952 | tf_op jit(solution)/shard_map/ppermute | solution.py:23
  17.0 4.0 %collective-permute-start.3 = (bf16[4,128,768]{2,1,0:T(8,128)(2,1)S(1)}, bf16[4,128,768]{2,1,0:T(8,128)(2,1)S(1)}, u32[]{:S(2)}, u32[]{:S(2)}) collective-permute-start(bf16[4,128,768]{2,1,0:T(8,128)(2,1)S(1)} %pad_maximum_fusion.12), channel_id=1, source_target_pairs={{0,1},{1,0},{2,3},{3,2},{4,5},{5,4},{6,7},{7,6},{8,9},{9,8},{10,11... | collective-permute-start | bytes 2359304 | tf_op jit(solution)/shard_map/ppermute | solution.py:23
  17.3 4.0 %collective-permute-start.5 = (bf16[1536,384]{1,0:T(8,128)(2,1)S(1)}, bf16[1536,384]{1,0:T(8,128)(2,1)S(1)}, u32[]{:S(2)}, u32[]{:S(2)}) collective-permute-start(bf16[1536,384]{1,0:T(8,128)(2,1)S(1)} %get-tuple-element.64), channel_id=1, source_target_pairs={{0,1},{1,0},{2,3},{3,2},{4,5},{5,4},{6,7},{7,6},{8,9},{9,8},{10,11... | collective-permute-start | bytes 3538952 | tf_op jit(solution)/shard_map/ppermute | solution.py:23
  17.9 10.1 %collective-permute-start.8 = (bf16[4,32,768]{2,1,0:T(8,128)(2,1)}, bf16[4,32,768]{2,1,0:T(8,128)(2,1)S(1)}, u32[]{:S(2)}, u32[]{:S(2)}) collective-permute-start(bf16[4,32,768]{2,1,0:T(8,128)(2,1)} %fusion.35), channel_id=1, source_target_pairs={{0,16},{16,0},{1,17},{17,1},{2,18},{18,2},{3,19},{19,3},{4,20},{20... | collective-permute-start | bytes 589832 | tf_op jit(solution)/shard_map/ppermute | solution.py:23
  21.1 15.1 %copy-start.2 = (bf16[4,128,384]{2,1,0:T(8,128)(2,1)}, bf16[4,128,384]{2,1,0:T(8,128)(2,1)S(1)}, u32[]{:S(2)}) copy-start(bf16[4,128,384]{2,1,0:T(8,128)(2,1)S(1)} %get-tuple-element.84) | copy-start | bytes 1179652
  21.5 14.7 %copy-start = (bf16[1536,768]{1,0:T(8,128)(2,1)}, bf16[1536,768]{1,0:T(8,128)(2,1)S(1)}, u32[]{:S(2)}) copy-start(bf16[1536,768]{1,0:T(8,128)(2,1)S(1)} %pad_maximum_fusion.1) | copy-start | bytes 7077892
  22.0 13.2 %collective-permute-start.6 = (bf16[128,1536]{1,0:T(8,128)(2,1)S(1)}, bf16[128,1536]{1,0:T(8,128)(2,1)S(1)}, u32[]{:S(2)}, u32[]{:S(2)}) collective-permute-start(bf16[128,1536]{1,0:T(8,128)(2,1)S(1)} %convolution_convert_fusion.7), channel_id=1, source_target_pairs={{0,2},{2,4},{4,6},{6,0},{1,3},{3,5},{5,7},{7,1},{8,10},{10,12},{12... | collective-permute-start | bytes 1179656 | tf_op jit(solution)/shard_map/ppermute | solution.py:23
  24.9 10.8 %collective-permute-start.7 = (bf16[128,1536]{1,0:T(8,128)(2,1)S(1)}, bf16[128,1536]{1,0:T(8,128)(2,1)S(1)}, u32[]{:S(2)}, u32[]{:S(2)}) collective-permute-start(bf16[128,1536]{1,0:T(8,128)(2,1)S(1)} %convolution_convert_fusion.6), channel_id=1, source_target_pairs={{0,6},{2,0},{4,2},{6,4},{1,7},{3,1},{5,3},{7,5},{8,14},{10,8},{12,... | collective-permute-start | bytes 1179656 | tf_op jit(solution)/shard_map/ppermute | solution.py:23
  28.0 11.1 %collective-permute-start.11 = (bf16[4,32,768]{2,1,0:T(8,128)(2,1)S(1)}, bf16[4,32,768]{2,1,0:T(8,128)(2,1)S(1)}, u32[]{:S(2)}, u32[]{:S(2)}) collective-permute-start(bf16[4,32,768]{2,1,0:T(8,128)(2,1)S(1)} %collective-permute-done.8), channel_id=1, source_target_pairs={{0,96},{32,0},{64,32},{96,64},{1,97},{33,1},{65,33},{97,65},{2,98}... | collective-permute-start | bytes 589832 | tf_op jit(solution)/shard_map/ppermute | solution.py:23
  30.1 9.4 %collective-permute-start.12 = (bf16[4,32,768]{2,1,0:T(8,128)(2,1)S(1)}, bf16[4,32,768]{2,1,0:T(8,128)(2,1)S(1)}, u32[]{:S(2)}, u32[]{:S(2)}) collective-permute-start(bf16[4,32,768]{2,1,0:T(8,128)(2,1)S(1)} %collective-permute-done.8), channel_id=1, source_target_pairs={{0,64},{32,96},{64,0},{96,32},{1,65},{33,97},{65,1},{97,33},{2,66}... | collective-permute-start | bytes 589832 | tf_op jit(solution)/shard_map/ppermute | solution.py:23
  31.3 10.7 %collective-permute-start.13 = (bf16[4,32,768]{2,1,0:T(8,128)(2,1)S(1)}, bf16[4,32,768]{2,1,0:T(8,128)(2,1)S(1)}, u32[]{:S(2)}, u32[]{:S(2)}) collective-permute-start(bf16[4,32,768]{2,1,0:T(8,128)(2,1)S(1)} %collective-permute-done.8), channel_id=1, source_target_pairs={{0,32},{32,64},{64,96},{96,0},{1,33},{33,65},{65,97},{97,1},{2,34}... | collective-permute-start | bytes 589832 | tf_op jit(solution)/shard_map/ppermute | solution.py:23
  44.7 7.4 %collective-permute-start.14 = (bf16[4,128,768]{2,1,0:T(8,128)(2,1)}, bf16[4,128,768]{2,1,0:T(8,128)(2,1)}, u32[]{:S(2)}, u32[]{:S(2)}) collective-permute-start(bf16[4,128,768]{2,1,0:T(8,128)(2,1)} %constant_dynamic-update-slice_fusion), channel_id=1, source_target_pairs={{0,1},{1,0},{2,3},{3,2},{4,5},{5,4},{6,7},{7,6},{8,9},{9,8},{10,11... | collective-permute-start | bytes 2359304 | tf_op jit(solution)/shard_map/ppermute | solution.py:23
  44.8 1.8 copy-start.1
  44.8 1.8 copy-start.3
  46.6 1.1 copy-start.6
  46.6 1.4 copy-start.5
  47.7 21.5 %collective-permute-start.9 = (bf16[128,3072]{1,0:T(8,128)(2,1)S(1)}, bf16[128,3072]{1,0:T(8,128)(2,1)S(1)}, u32[]{:S(2)}, u32[]{:S(2)}) collective-permute-start(bf16[128,3072]{1,0:T(8,128)(2,1)S(1)} %copy-done.6), channel_id=1, source_target_pairs={{0,2},{2,4},{4,6},{6,0},{1,3},{3,5},{5,7},{7,1},{8,10},{10,12},{12... | collective-permute-start | bytes 2359304 | tf_op jit(solution)/shard_map/ppermute | solution.py:23
  47.9 21.3 %collective-permute-start.10 = (bf16[128,3072]{1,0:T(8,128)(2,1)S(1)}, bf16[128,3072]{1,0:T(8,128)(2,1)S(1)}, u32[]{:S(2)}, u32[]{:S(2)}) collective-permute-start(bf16[128,3072]{1,0:T(8,128)(2,1)S(1)} %copy-done.5), channel_id=1, source_target_pairs={{0,6},{2,0},{4,2},{6,4},{1,7},{3,1},{5,3},{7,5},{8,14},{10,8},{12,... | collective-permute-start | bytes 2359304 | tf_op jit(solution)/shard_map/ppermute | solution.py:23
  53.8 23.4 %collective-permute-start.16 = (bf16[128,1536]{1,0:T(8,128)(2,1)S(1)}, bf16[128,1536]{1,0:T(8,128)(2,1)S(1)}, u32[]{:S(2)}, u32[]{:S(2)}) collective-permute-start(bf16[128,1536]{1,0:T(8,128)(2,1)S(1)} %convolution_convert_fusion.3), channel_id=1, source_target_pairs={{0,2},{2,4},{4,6},{6,0},{1,3},{3,5},{5,7},{7,1},{8,10},{10,12},{12... | collective-permute-start | bytes 1179656 | tf_op jit(solution)/shard_map/ppermute | solution.py:23
  54.8 22.5 %collective-permute-start.17 = (bf16[128,1536]{1,0:T(8,128)(2,1)S(1)}, bf16[128,1536]{1,0:T(8,128)(2,1)S(1)}, u32[]{:S(2)}, u32[]{:S(2)}) collective-permute-start(bf16[128,1536]{1,0:T(8,128)(2,1)S(1)} %convolution_convert_fusion.2), channel_id=1, source_target_pairs={{0,6},{2,0},{4,2},{6,4},{1,7},{3,1},{5,3},{7,5},{8,14},{10,8},{12,... | collective-permute-start | bytes 1179656 | tf_op jit(solution)/shard_map/ppermute | solution.py:23
  70.4 18.8 %collective-permute-start.15 = (bf16[128,3072]{1,0:T(8,128)(2,1)S(1)}, bf16[128,3072]{1,0:T(8,128)(2,1)S(1)}, u32[]{:S(2)}, u32[]{:S(2)}) collective-permute-start(bf16[128,3072]{1,0:T(8,128)(2,1)S(1)} %pad_maximum_fusion.15), channel_id=1, source_target_pairs={{0,8},{8,0},{1,9},{9,1},{2,10},{10,2},{3,11},{11,3},{4,12},{12,4},... | collective-permute-start | bytes 2359304 | tf_op jit(solution)/shard_map/ppermute | solution.py:23
  77.9 21.7 %collective-permute-start.20 = (bf16[128,3072]{1,0:T(8,128)(2,1)S(1)}, bf16[128,3072]{1,0:T(8,128)(2,1)S(1)}, u32[]{:S(2)}, u32[]{:S(2)}) collective-permute-start(bf16[128,3072]{1,0:T(8,128)(2,1)S(1)} %pad_maximum_fusion.16), channel_id=1, source_target_pairs={{0,2},{2,4},{4,6},{6,0},{1,3},{3,5},{5,7},{7,1},{8,10},{10,12},{12... | collective-permute-start | bytes 2359304 | tf_op jit(solution)/shard_map/ppermute | solution.py:23
  79.4 20.8 %collective-permute-start.21 = (bf16[128,3072]{1,0:T(8,128)(2,1)S(1)}, bf16[128,3072]{1,0:T(8,128)(2,1)S(1)}, u32[]{:S(2)}, u32[]{:S(2)}) collective-permute-start(bf16[128,3072]{1,0:T(8,128)(2,1)S(1)} %pad_maximum_fusion.17), channel_id=1, source_target_pairs={{0,6},{2,0},{4,2},{6,4},{1,7},{3,1},{5,3},{7,5},{8,14},{10,8},{12,... | collective-permute-start | bytes 2359304 | tf_op jit(solution)/shard_map/ppermute | solution.py:23
  90.0 25.5 %collective-permute-start.18 = (bf16[128,3072]{1,0:T(8,128)(2,1)S(1)}, bf16[128,3072]{1,0:T(8,128)(2,1)S(1)}, u32[]{:S(2)}, u32[]{:S(2)}) collective-permute-start(bf16[128,3072]{1,0:T(8,128)(2,1)S(1)} %pad_maximum_fusion.18), channel_id=1, source_target_pairs={{0,6},{2,0},{4,2},{6,4},{1,7},{3,1},{5,3},{7,5},{8,14},{10,8},{12,... | collective-permute-start | bytes 2359304 | tf_op jit(solution)/shard_map/ppermute | solution.py:23
  92.7 22.8 %collective-permute-start.19 = (bf16[128,3072]{1,0:T(8,128)(2,1)S(1)}, bf16[128,3072]{1,0:T(8,128)(2,1)S(1)}, u32[]{:S(2)}, u32[]{:S(2)}) collective-permute-start(bf16[128,3072]{1,0:T(8,128)(2,1)S(1)} %pad_maximum_fusion.18), channel_id=1, source_target_pairs={{0,2},{2,4},{4,6},{6,0},{1,3},{3,5},{5,7},{7,1},{8,10},{10,12},{12... | collective-permute-start | bytes 2359304 | tf_op jit(solution)/shard_map/ppermute | solution.py:23
  100.9 18.6 %collective-permute-start.24 = (bf16[128,3072]{1,0:T(8,128)(2,1)S(1)}, bf16[128,3072]{1,0:T(8,128)(2,1)S(1)}, u32[]{:S(2)}, u32[]{:S(2)}) collective-permute-start(bf16[128,3072]{1,0:T(8,128)(2,1)S(1)} %pad_maximum_fusion.19), channel_id=1, source_target_pairs={{0,8},{8,0},{1,9},{9,1},{2,10},{10,2},{3,11},{11,3},{4,12},{12,4},... | collective-permute-start | bytes 2359304 | tf_op jit(solution)/shard_map/ppermute | solution.py:23
  115.5 13.3 %collective-permute-start.22 = (bf16[128,1536]{1,0:T(8,128)(2,1)S(1)}, bf16[128,1536]{1,0:T(8,128)(2,1)S(1)}, u32[]{:S(2)}, u32[]{:S(2)}) collective-permute-start(bf16[128,1536]{1,0:T(8,128)(2,1)S(1)} %get-tuple-element.78), channel_id=1, source_target_pairs={{0,6},{2,0},{4,2},{6,4},{1,7},{3,1},{5,3},{7,5},{8,14},{10,8},{12,... | collective-permute-start | bytes 1179656 | tf_op jit(solution)/shard_map/ppermute | solution.py:23
  119.4 13.3 %collective-permute-start.23 = (bf16[128,1536]{1,0:T(8,128)(2,1)S(1)}, bf16[128,1536]{1,0:T(8,128)(2,1)S(1)}, u32[]{:S(2)}, u32[]{:S(2)}) collective-permute-start(bf16[128,1536]{1,0:T(8,128)(2,1)S(1)} %get-tuple-element.74), channel_id=1, source_target_pairs={{0,2},{2,4},{4,6},{6,0},{1,3},{3,5},{5,7},{7,1},{8,10},{10,12},{12... | collective-permute-start | bytes 1179656 | tf_op jit(solution)/shard_map/ppermute | solution.py:23
  120.2 23.0 %collective-permute-start.26 = (bf16[128,3072]{1,0:T(8,128)(2,1)S(1)}, bf16[128,3072]{1,0:T(8,128)(2,1)S(1)}, u32[]{:S(2)}, u32[]{:S(2)}) collective-permute-start(bf16[128,3072]{1,0:T(8,128)(2,1)S(1)} %pad_maximum_fusion.20), channel_id=1, source_target_pairs={{0,6},{2,0},{4,2},{6,4},{1,7},{3,1},{5,3},{7,5},{8,14},{10,8},{12,... | collective-permute-start | bytes 2359304 | tf_op jit(solution)/shard_map/ppermute | solution.py:23
  123.5 23.3 %collective-permute-start.27 = (bf16[128,3072]{1,0:T(8,128)(2,1)S(1)}, bf16[128,3072]{1,0:T(8,128)(2,1)S(1)}, u32[]{:S(2)}, u32[]{:S(2)}) collective-permute-start(bf16[128,3072]{1,0:T(8,128)(2,1)S(1)} %pad_maximum_fusion.20), channel_id=1, source_target_pairs={{0,2},{2,4},{4,6},{6,0},{1,3},{3,5},{5,7},{7,1},{8,10},{10,12},{12... | collective-permute-start | bytes 2359304 | tf_op jit(solution)/shard_map/ppermute | solution.py:23
  134.2 15.9 %collective-permute-start.25 = (f32[512,384]{1,0:T(8,128)S(1)}, f32[512,384]{1,0:T(8,128)S(1)}, u32[]{:S(2)}, u32[]{:S(2)}) collective-permute-start(f32[512,384]{1,0:T(8,128)S(1)} %slice.304), channel_id=1, source_target_pairs={{0,1},{1,0},{2,3},{3,2},{4,5},{5,4},{6,7},{7,6},{8,9},{9,8},{10,11... | collective-permute-start | bytes 2359304 | tf_op jit(solution)/shard_map/ppermute | solution.py:23
  146.8 8.4 %collective-permute-start.31 = (bf16[128,1536]{1,0:T(8,128)(2,1)S(1)}, bf16[128,1536]{1,0:T(8,128)(2,1)S(1)}, u32[]{:S(2)}, u32[]{:S(2)}) collective-permute-start(bf16[128,1536]{1,0:T(8,128)(2,1)S(1)} %get-tuple-element.76), channel_id=1, source_target_pairs={{0,6},{2,0},{4,2},{6,4},{1,7},{3,1},{5,3},{7,5},{8,14},{10,8},{12,... | collective-permute-start | bytes 1179656 | tf_op jit(solution)/shard_map/ppermute | solution.py:23
  147.1 9.8 %collective-permute-start.32 = (bf16[128,1536]{1,0:T(8,128)(2,1)S(1)}, bf16[128,1536]{1,0:T(8,128)(2,1)S(1)}, u32[]{:S(2)}, u32[]{:S(2)}) collective-permute-start(bf16[128,1536]{1,0:T(8,128)(2,1)S(1)} %get-tuple-element.72), channel_id=1, source_target_pairs={{0,2},{2,4},{4,6},{6,0},{1,3},{3,5},{5,7},{7,1},{8,10},{10,12},{12... | collective-permute-start | bytes 1179656 | tf_op jit(solution)/shard_map/ppermute | solution.py:23
  158.4 4.5 %collective-permute-start.33 = (f32[512,384]{1,0:T(8,128)S(1)}, f32[512,384]{1,0:T(8,128)S(1)}, u32[]{:S(2)}, u32[]{:S(2)}) collective-permute-start(f32[512,384]{1,0:T(8,128)S(1)} %slice.310), channel_id=1, source_target_pairs={{0,1},{1,0},{2,3},{3,2},{4,5},{5,4},{6,7},{7,6},{8,9},{9,8},{10,11... | collective-permute-start | bytes 2359304 | tf_op jit(solution)/shard_map/ppermute | solution.py:23
  159.4 8.7 %collective-permute-start.30 = (bf16[4,32,384]{2,1,0:T(8,128)(2,1)S(1)}, bf16[4,32,384]{2,1,0:T(8,128)(2,1)S(1)}, u32[]{:S(2)}, u32[]{:S(2)}) collective-permute-start(bf16[4,32,384]{2,1,0:T(8,128)(2,1)S(1)} %get-tuple-element.88), channel_id=1, source_target_pairs={{0,96},{32,0},{64,32},{96,64},{1,97},{33,1},{65,33},{97,65},{2,98}... | collective-permute-start | bytes 294920 | tf_op jit(solution)/shard_map/ppermute | solution.py:23
  160.1 9.3 %collective-permute-start.29 = (bf16[4,32,384]{2,1,0:T(8,128)(2,1)S(1)}, bf16[4,32,384]{2,1,0:T(8,128)(2,1)S(1)}, u32[]{:S(2)}, u32[]{:S(2)}) collective-permute-start(bf16[4,32,384]{2,1,0:T(8,128)(2,1)S(1)} %get-tuple-element.89), channel_id=1, source_target_pairs={{0,64},{32,96},{64,0},{96,32},{1,65},{33,97},{65,1},{97,33},{2,66}... | collective-permute-start | bytes 294920 | tf_op jit(solution)/shard_map/ppermute | solution.py:23
  161.3 11.8 %collective-permute-start.28 = (bf16[4,32,384]{2,1,0:T(8,128)(2,1)S(1)}, bf16[4,32,384]{2,1,0:T(8,128)(2,1)S(1)}, u32[]{:S(2)}, u32[]{:S(2)}) collective-permute-start(bf16[4,32,384]{2,1,0:T(8,128)(2,1)S(1)} %get-tuple-element.87), channel_id=1, source_target_pairs={{0,32},{32,64},{64,96},{96,0},{1,33},{33,65},{65,97},{97,1},{2,34}... | collective-permute-start | bytes 294920 | tf_op jit(solution)/shard_map/ppermute | solution.py:23
  162.8 17.3 %collective-permute-start.38 = (bf16[384,1536]{1,0:T(8,128)(2,1)S(1)}, bf16[384,1536]{1,0:T(8,128)(2,1)S(1)}, u32[]{:S(2)}, u32[]{:S(2)}) collective-permute-start(bf16[384,1536]{1,0:T(8,128)(2,1)S(1)} %fusion.1), channel_id=1, source_target_pairs={{0,1},{1,0},{2,3},{3,2},{4,5},{5,4},{6,7},{7,6},{8,9},{9,8},{10,11... | collective-permute-start | bytes 3538952 | tf_op jit(solution)/shard_map/ppermute | solution.py:23
  163.1 11.5 %collective-permute-start.37 = (bf16[4,32,384]{2,1,0:T(8,128)(2,1)S(1)}, bf16[4,32,384]{2,1,0:T(8,128)(2,1)S(1)}, u32[]{:S(2)}, u32[]{:S(2)}) collective-permute-start(bf16[4,32,384]{2,1,0:T(8,128)(2,1)S(1)} %get-tuple-element.93), channel_id=1, source_target_pairs={{0,112},{16,96},{32,16},{48,0},{64,48},{80,32},{96,80},{112,64},{1... | collective-permute-start | bytes 294920 | tf_op jit(solution)/shard_map/ppermute | solution.py:162
  168.1 10.7 %collective-permute-start.36 = (bf16[4,32,384]{2,1,0:T(8,128)(2,1)S(1)}, bf16[4,32,384]{2,1,0:T(8,128)(2,1)S(1)}, u32[]{:S(2)}, u32[]{:S(2)}) collective-permute-start(bf16[4,32,384]{2,1,0:T(8,128)(2,1)S(1)} %get-tuple-element.91), channel_id=1, source_target_pairs={{0,80},{16,64},{32,112},{48,96},{64,16},{80,0},{96,48},{112,32},{1... | collective-permute-start | bytes 294920 | tf_op jit(solution)/shard_map/ppermute | solution.py:162
  169.3 9.7 %collective-permute-start.35 = (bf16[4,32,384]{2,1,0:T(8,128)(2,1)S(1)}, bf16[4,32,384]{2,1,0:T(8,128)(2,1)S(1)}, u32[]{:S(2)}, u32[]{:S(2)}) collective-permute-start(bf16[4,32,384]{2,1,0:T(8,128)(2,1)S(1)} %get-tuple-element.92), channel_id=1, source_target_pairs={{0,48},{16,32},{32,80},{48,64},{64,112},{80,96},{96,16},{112,0},{1... | collective-permute-start | bytes 294920 | tf_op jit(solution)/shard_map/ppermute | solution.py:162
  173.1 6.2 %collective-permute-start.34 = (bf16[4,32,384]{2,1,0:T(8,128)(2,1)S(1)}, bf16[4,32,384]{2,1,0:T(8,128)(2,1)S(1)}, u32[]{:S(2)}, u32[]{:S(2)}) collective-permute-start(bf16[4,32,384]{2,1,0:T(8,128)(2,1)S(1)} %get-tuple-element.90), channel_id=1, source_target_pairs={{0,16},{16,0},{32,48},{48,32},{64,80},{80,64},{96,112},{112,96},{1... | collective-permute-start | bytes 294920 | tf_op jit(solution)/shard_map/ppermute | solution.py:162
  174.6 8.1 %collective-permute-start.39 = (bf16[1536,384]{1,0:T(8,128)(2,1)S(1)}, bf16[1536,384]{1,0:T(8,128)(2,1)S(1)}, u32[]{:S(2)}, u32[]{:S(2)}) collective-permute-start(bf16[1536,384]{1,0:T(8,128)(2,1)S(1)} %fusion.3), channel_id=1, source_target_pairs={{0,1},{1,0},{2,3},{3,2},{4,5},{5,4},{6,7},{7,6},{8,9},{9,8},{10,11... | collective-permute-start | bytes 3538952 | tf_op jit(solution)/shard_map/ppermute | solution.py:23
where the time goes:
time: 186 us; the launch traced here: 185 us
  waiting for transfers between devices  84.7 us (46%)
  starting transfers between devices  56.7 us (30%)
  matrix products  21.3 us (11%)
  other arithmetic  12.6 us (7%)
  local copies, waits for them, and re-layouts  8.9 us (5%)
    ppermute x36, waiting for transfers between devices, shift(): return lax.ppermute(x, axis, [(i, (i + by) % n) for i in range(n)])  80.1 us
    ppermute x36, starting transfers between devices, shift(): return lax.ppermute(x, axis, [(i, (i + by) % n) for i in range(n)])  46.2 us
    dot_general x26, matrix products, dot(): lax.dot_general(a, b, (((da,), (db,)), ((), ())), preferred_element_type=...  21.3 us
    ppermute x4, starting transfers between devices, local(): lax.ppermute(back_b[:, d], ROWS, [(i, (i // 2 + d) % 4 * 2 + (i + 1) % 2)...  10.5 us
    ppermute x4, waiting for transfers between devices, local(): lax.ppermute(back_b[:, d], ROWS, [(i, (i // 2 + d) % 4 * 2 + (i + 1) % 2)...  4.6 us
  transfers between devices with their start and end apart: 40, of which 21 were waited for; matrix products, arithmetic and copies ran while one was open for 18% of the time, Pallas kernels for 0%

commit v1 on v0

--- a/solution.py
+++ b/solution.py
@@ -1,6 +1,8 @@
 import jax
 import jax.numpy as jnp
 from jax import lax
+from jax.experimental import pallas as pl
+from jax.experimental.pallas import tpu as pltpu
 from jax.sharding import Mesh
 from jax.sharding import PartitionSpec as P
 
@@ -31,6 +33,56 @@
     return jnp.concatenate([jnp.where(flag == 0, first, second), jnp.where(flag == 0, second, first)], axis)
 
 
+CHEAP = dict(
+    cost_estimate=pl.CostEstimate(flops=10**6, bytes_accessed=10**5, transcendentals=0),
+    compiler_params=pltpu.CompilerParams(vmem_limit_bytes=24 * 2**20),
+)
+
+
+def products(tok, cot, wi, wo):
+    rows, feat = tok.shape
+    hid = wi.shape[1]
+    block = hid // 3
+
+    def body(tok, cot, wi, wo, p, g):
+        p[...] = jnp.dot(tok[...], wi[...], preferred_element_type=F32)
+        g[...] = dot(cot[...], wo[...], 1, 1)
+
+    whole = pl.BlockSpec((rows, feat), lambda i: (0, 0))
+    out = pl.BlockSpec((rows, block), lambda i: (0, i))
+    return pl.pallas_call(
+        body,
+        grid=(3,),
+        in_specs=[
+            whole,
+            whole,
+            pl.BlockSpec((feat, block), lambda i: (0, i)),
+            pl.BlockSpec((block, feat), lambda i: (i, 0)),
+        ],
+        out_specs=[out, out],
+        out_shape=[jax.ShapeDtypeStruct((rows, hid), F32)] * 2,
+        **CHEAP,
+    )(tok, cot, wi, wo)
+
+
+def input_product(grad, wi):
+    rows, hid = grad.shape
+    feat = wi.shape[0]
+    block = rows // 2
+
+    def body(grad, wi, out):
+        out[...] = dot(grad[...], wi[...], 1, 1)
+
+    return pl.pallas_call(
+        body,
+        grid=(2,),
+        in_specs=[pl.BlockSpec((block, hid), lambda i: (i, 0)), pl.BlockSpec((feat, hid), lambda i: (0, 0))],
+        out_specs=pl.BlockSpec((block, feat), lambda i: (i, 0)),
+        out_shape=jax.ShapeDtypeStruct((rows, feat), F32),
+        **CHEAP,
+    )(grad, wi)
+
+
 def gate(value, *after):
     return lax.optimization_barrier((value, after))[0]
 
@@ -60,18 +112,19 @@
     def up_down(up, down):
         return shift(up, "z", 1), shift(down, "z", -1)
 
-    def step1(tok, cot):
-        return dot(tok[2], wi, 1, 0).astype(BF16), dot(cot[2], wo, 1, 1).astype(BF16)
-
-    def step2(tok, cot, up, down):
-        return (
-            cat(dot(tok[1], wi, 1, 0) + up.astype(F32), dot(cot[1], wo, 1, 1)),
-            cat(dot(tok[3], wi, 1, 0), dot(cot[3], wo, 1, 1) + down.astype(F32)),
-        )
-
-    def step3(tok, cot, up, down):
-        p = dot(tok[0], wi, 1, 0) + up[:, :hid].astype(F32) + down[:, :hid].astype(F32)
-        g = dot(cot[0], wo, 1, 1) + up[:, hid:].astype(F32) + down[:, hid:].astype(F32)
+    def partial_sums(tok, cot):
+        p, g = products(tok.reshape(4 * rows, -1), cot.reshape(4 * rows, -1), wi, wo)
+        return p.reshape(4, rows, hid), g.reshape(4, rows, hid)
+
+    def step1(p, g):
+        return p[2].astype(BF16), g[2].astype(BF16)
+
+    def step2(p, g, up, down):
+        return cat(p[1] + up.astype(F32), g[1]), cat(p[3], g[3] + down.astype(F32))
+
+    def step3(p, g, up, down):
+        p = p[0] + up[:, :hid].astype(F32) + down[:, :hid].astype(F32)
+        g = g[0] + up[:, hid:].astype(F32) + down[:, hid:].astype(F32)
         return p, g, cat(p, g)
 
     def step4(p, g, other):
@@ -92,50 +145,51 @@
         return act, grad
 
     def input_part(grad):
-        part = dot(grad, wi, 1, 1)
+        part = input_product(grad, wi)
         return part[:, :feat], part[:, feat:]
 
     def by_row(mine, other):
         return (mine + other).reshape(4, -1, piece, feat)
 
     own = relative(jnp.concatenate([tokens, cotangent], 1), -1)
+    across = shift(own, "xh", 1)
     near = [own] + [shift(own, "y", -d) for d in (1, 2, 3)]
     wi_keep, wi_send = halves(w_in, 1)
     wo_keep, wo_send = halves(w_out, 0)
     wi_got, wo_got = shift(wi_send, "core", 1), shift(wo_send, "core", 1)
-    across = shift(own, "xh", 1)
-    near = jnp.concatenate(near, 1)
+    across = gate(across, wi_send, wo_send)
+    far = [across] + [shift(across, "y", -d) for d in (1, 2, 3)]
+    near = jnp.concatenate(gate(near, across), 1)
     near_other = shift(near, "core", 1)
     wi = jnp.concatenate([wi_keep, wi_got], 0)
     wo = jnp.concatenate([wo_keep, wo_got], 1)
     wi, wo = lax.optimization_barrier((wi, wo))
 
     tok_a, cot_a = features(near, near_other)
-    m_a = step1(tok_a, cot_a)
-    r_a = up_down(*m_a)
-
-    across = gate(across, m_a)
-    far = [across] + [shift(across, "y", -d) for d in (1, 2, 3)]
-
-    m_a = step2(tok_a, cot_a, *gate(r_a, across))
+    pg_a = partial_sums(tok_a, cot_a)
+    m_a = step1(*pg_a)
     r_a = up_down(*m_a)
 
     far = jnp.concatenate(gate(far, m_a), 1)
     far_other = shift(far, "core", 1)
     tok_b, cot_b = features(far, far_other)
-    m_b = step1(tok_b, cot_b)
+    pg_b = partial_sums(tok_b, cot_b)
+    m_b = step1(*pg_b)
     r_b = up_down(*m_b)
 
-    p_a, g_a, m_a = step3(tok_a, cot_a, *gate(r_a, m_b))
+    m_a = step2(*pg_a, *gate(r_a, m_b))
+    r_a = up_down(*m_a)
+
+    p_a, g_a, m_a = step3(*pg_a, *r_a)
     x_a = shift(m_a, "xl", 1)
 
-    m_b = step2(tok_b, cot_b, *gate(r_b, m_a))
+    m_b = step2(*pg_b, *gate(r_b, m_a))
     r_b = up_down(*m_b)
 
     mine_a = step4(p_a, g_a, gate(x_a, m_b))
     s_a = send_mine(mine_a)
 
-    p_b, g_b, m_b = step3(tok_b, cot_b, *gate(r_b, mine_a))
+    p_b, g_b, m_b = step3(*pg_b, *gate(r_b, mine_a))
     x_b = shift(m_b, "xl", 1)
 
     s_a = gate(s_a, m_b)
@@ -148,17 +202,17 @@
     in_a, in_a_other = input_part(grad_a)
     in_a_got = shift(in_a_other, "core", 1)
 
-    s_b = gate(s_b, in_a_other)
+    back_a = by_row(in_a, in_a_got)
+    back = [shift(back_a[:, d].astype(BF16), "y", d) for d in (1, 2, 3)]
+
+    s_b = gate(s_b, back_a)
     t_b = send_on(*s_b)
 
-    back_a = by_row(in_a, gate(in_a_got, s_b))
-    back = [shift(back_a[:, d].astype(BF16), "y", d) for d in (1, 2, 3)]
-
-    act_b, grad_b = gathered(mine_b, *s_b, *gate(t_b, back_a))
+    act_b, grad_b = gathered(mine_b, *s_b, *gate(t_b, back))
     in_b, in_b_other = input_part(grad_b)
     in_b_got = shift(in_b_other, "core", 1)
     back_b = by_row(in_b, in_b_got).astype(BF16)
-    back += [
+    back_far = [
         lax.ppermute(back_b[:, d], ROWS, [(i, ((i // 2 + d) % 4) * 2 + (i + 1) % 2) for i in range(8)])
         for d in (0, 1, 2, 3)
     ]
@@ -167,9 +221,9 @@
         return (dot(left[0], right[0], 0, 0) + dot(left[1], right[1], 0, 0)).astype(BF16)
 
     flat = lambda a: a.reshape(-1, a.shape[-1])
+    grads, acts = gate(([grad_a, grad_b], [act_a, act_b]), in_b_other)
     toks = [flat(a) for a in (tok_a, tok_b)]
     cots = [flat(a) for a in (cot_a, cot_b)]
-    grads, acts = [grad_a, grad_b], [act_a, act_b]
     wi_other = shift(token_sum([t[:, feat:] for t in toks], grads), "core", 1)
     wo_other = shift(token_sum(acts, [c[:, feat:] for c in cots]), "core", 1)
     wi_own = token_sum([t[:, :feat] for t in toks], grads)
@@ -178,7 +232,7 @@
     w_out_grad = swap_halves(wo_own, wo_other, core, 0)
 
     total = back_a[:, 0]
-    for part in back:
+    for part in back + gate(back_far, w_in_grad, w_out_grad):
         total = total + part.astype(F32)
     input_grad = relative(total, 1).reshape(rows, feat).astype(BF16)
     return (input_grad, w_in_grad, w_out_grad)

time: 186 us -> 193 us (1.038)
  waiting for transfers between devices: 84.7 us -> 101 us
  matrix products: 21.3 us -> 7.31 us
  Pallas kernels: 0 us -> 10.3 us
  starting transfers between devices: 56.7 us -> 49.9 us
    ppermute x36, waiting for transfers between devices: 80.1 us -> 101 us  [shift(): return lax.ppermute(x, axis, [(i, (i + by) % n) for i in range(n)])]
    dot_general x26 -> x8, matrix products: 21.3 us -> 7.31 us  [dot(): lax.dot_general(a, b, (((da,), (db,)), ((), ())), preferred_element_type=...]
    pallas_call x0 -> x4, Pallas kernels: none -> 10.3 us  [the longest x2 7.06 us: products(): pl.pallas_call(body, grid=(3,), in_specs=[whole, whole, pl.BlockSpec((fea...]
    ppermute x36, starting transfers between devices: 46.2 us -> 41.2 us  [shift(): return lax.ppermute(x, axis, [(i, (i + by) % n) for i in range(n)])]
    ppermute x4, waiting for transfers between devices: 4.6 us -> 0.1 us  [local(): lax.ppermute(back_b[:, d], ROWS, [(i, (i // 2 + d) % 4 * 2 + (i + 1) % 2)...]
    slice x2, local copies, waits for them, and re-layouts: 0.1 us -> 2.08 us  [gathered(): below[:, :hid]]
  transfers between devices with their start and end apart: 40 -> 40, of which waited for: 21 -> 24; matrix products, arithmetic and copies ran while one was open for 18% -> 12% of each run, Pallas kernels for 0% -> 4%
where the time goes in v1:
time: 193 us; the launch traced here: 192 us
  waiting for transfers between devices  101 us (52%)
  starting transfers between devices  49.9 us (26%)
  other arithmetic  12.4 us (6%)
  local copies, waits for them, and re-layouts  10.5 us (5%)
  Pallas kernels  10.3 us (5%)
  matrix products  7.31 us (4%)
    ppermute x36, waiting for transfers between devices, shift(): return lax.ppermute(x, axis, [(i, (i + by) % n) for i in range(n)])  101 us
    ppermute x36, starting transfers between devices, shift(): return lax.ppermute(x, axis, [(i, (i + by) % n) for i in range(n)])  41.2 us
    ppermute x4, starting transfers between devices, local(): lax.ppermute(back_b[:, d], ROWS, [(i, (i // 2 + d) % 4 * 2 + (i + 1) % 2)...  8.71 us
    dot_general x8, matrix products, dot(): lax.dot_general(a, b, (((da,), (db,)), ((), ())), preferred_element_type=...  7.31 us
    pallas_call x2, Pallas kernels, products(): pl.pallas_call(body, grid=(3,), in_specs=[whole, whole, pl.BlockSpec((fea...  7.06 us
  transfers between devices with their start and end apart: 40, of which 24 were waited for; matrix products, arithmetic and copies ran while one was open for 12% of the time, Pallas kernels for 4%

profile of v1, /device:TPU:0, one launch (start us, length us, event | category | flops | bytes accessed | tf_op | source)
XLA Modules:
  0.0 192.4 jit_solution(16343153997732347383)
XLA Ops:
  0.7 1.0 pad_maximum_fusion.20
  1.7 3.2 %collective-permute-start.3 = (bf16[4,32,768]{2,1,0:T(8,128)(2,1)S(1)}, bf16[4,32,768]{2,1,0:T(8,128)(2,1)S(1)}, u32[]{:S(2)}, u32[]{:S(2)}) collective-permute-start(bf16[4,32,768]{2,1,0:T(8,128)(2,1)S(1)} %fusion.31), channel_id=1, source_target_pairs={{0,16},{16,0},{1,17},{17,1},{2,18},{18,2},{3,19},{19,3},{4,20},{20... | collective-permute-start | bytes 589832 | tf_op jit(solution)/shard_map/ppermute | solution.py:25
  4.9 3.0 %collective-permute-start = (bf16[4,32,768]{2,1,0:T(8,128)(2,1)S(1)}, bf16[4,32,768]{2,1,0:T(8,128)(2,1)S(1)}, u32[]{:S(2)}, u32[]{:S(2)}) collective-permute-start(bf16[4,32,768]{2,1,0:T(8,128)(2,1)S(1)} %fusion.31), channel_id=1, source_target_pairs={{0,96},{32,0},{64,32},{96,64},{1,97},{33,1},{65,33},{97,65},{2,98}... | collective-permute-start | bytes 589832 | tf_op jit(solution)/shard_map/ppermute | solution.py:25
  8.6 1.0 collective-permute-start.2
  9.5 2.0 %constant_dynamic-slice_fusion = (bf16[1536,384]{1,0:T(8,128)(2,1)S(1)}, bf16[1536,384]{1,0:T(8,128)(2,1)S(1)}) fusion(bf16[3072,384]{1,0:T(8,128)(2,1)} %param.7, s32[]{:T(128)S(6)} %select_n.58, s32[]{:T(128)S(6)} %select_n.57), kind=kLoop, calls=%fused_computation.108 | loop fusion | bytes 4718600 | tf_op jit(solution)/shard_map/dynamic_slice | solution.py:100
  12.1 3.9 %collective-permute-done = bf16[4,32,768]{2,1,0:T(8,128)(2,1)S(1)} collective-permute-done((bf16[4,32,768]{2,1,0:T(8,128)(2,1)S(1)}, bf16[4,32,768]{2,1,0:T(8,128)(2,1)S(1)}, u32[]{:S(2)}, u32[]{:S(2)}) %collective-permute-start) | collective-permute-done | bytes 196640 | tf_op jit(solution)/shard_map/ppermute | solution.py:25
  16.0 1.3 collective-permute-done.1
  17.3 2.4 %collective-permute-done.2 = bf16[4,32,768]{2,1,0:T(8,128)(2,1)S(1)} collective-permute-done((bf16[4,32,768]{2,1,0:T(8,128)(2,1)S(1)}, bf16[4,32,768]{2,1,0:T(8,128)(2,1)S(1)}, u32[]{:S(2)}, u32[]{:S(2)}) %collective-permute-start.2) | collective-permute-done | bytes 196640 | tf_op jit(solution)/shard_map/ppermute | solution.py:25
  21.1 0.8 collective-permute-start.11
  22.2 2.4 %collective-permute-start.9 = (bf16[4,32,768]{2,1,0:T(8,128)(2,1)S(1)}, bf16[4,32,768]{2,1,0:T(8,128)(2,1)S(1)}, u32[]{:S(2)}, u32[]{:S(2)}) collective-permute-start(bf16[4,32,768]{2,1,0:T(8,128)(2,1)S(1)} %collective-permute-done.3), channel_id=1, source_target_pairs={{0,96},{32,0},{64,32},{96,64},{1,97},{33,1},{65,33},{97,65},{2,98}... | collective-permute-start | bytes 589832 | tf_op jit(solution)/shard_map/ppermute | solution.py:25
  25.7 3.5 %shard_map.67 = (f32[512,1536]{1,0:T(8,128)S(1)}, f32[512,1536]{1,0:T(8,128)S(1)}) custom-call(bf16[512,768]{1,0:T(8,128)(2,1)S(1)} %bitcast.52, bf16[512,768]{1,0:T(8,128)(2,1)S(1)} %bitcast.61, bf16[768,1536]{1,0:T(8,128)(2,1)S(1)} %pad_maximum_fusion.wi, bf16[1536,768]{1,0:T(8,128)(2,1)S(1)} %pad_maximum_fusion.1.wo), custom_call_target="tpu_custom_call" | custom-call | flops 1000000 | bytes 100000 | tf_op jit(solution)/shard_map/pallas_call | solution.py:53
  29.8 3.7 %collective-permute-done.11 = bf16[4,32,768]{2,1,0:T(8,128)(2,1)S(1)} collective-permute-done((bf16[4,32,768]{2,1,0:T(8,128)(2,1)S(1)}, bf16[4,32,768]{2,1,0:T(8,128)(2,1)S(1)}, u32[]{:S(2)}, u32[]{:S(2)}) %collective-permute-start.11) | collective-permute-done | bytes 196640 | tf_op jit(solution)/shard_map/ppermute | solution.py:25
  33.7 2.0 %collective-permute-start.7 = (bf16[128,1536]{1,0:T(8,128)(2,1)S(1)}, bf16[128,1536]{1,0:T(8,128)(2,1)S(1)}, u32[]{:S(2)}, u32[]{:S(2)}) collective-permute-start(bf16[128,1536]{1,0:T(8,128)(2,1)S(1)} %get-tuple-element.104), channel_id=1, source_target_pairs={{0,2},{2,4},{4,6},{6,0},{1,3},{3,5},{5,7},{7,1},{8,10},{10,12},{12... | collective-permute-start | bytes 1179656 | tf_op jit(solution)/shard_map/ppermute | solution.py:25
  35.6 2.2 %collective-permute-start.8 = (bf16[128,1536]{1,0:T(8,128)(2,1)S(1)}, bf16[128,1536]{1,0:T(8,128)(2,1)S(1)}, u32[]{:S(2)}, u32[]{:S(2)}) collective-permute-start(bf16[128,1536]{1,0:T(8,128)(2,1)S(1)} %get-tuple-element.102), channel_id=1, source_target_pairs={{0,6},{2,0},{4,2},{6,4},{1,7},{3,1},{5,3},{7,5},{8,14},{10,8},{12,... | collective-permute-start | bytes 1179656 | tf_op jit(solution)/shard_map/ppermute | solution.py:25
  38.2 3.5 %shard_map.68 = (f32[512,1536]{1,0:T(8,128)S(1)}, f32[512,1536]{1,0:T(8,128)S(1)}) custom-call(bf16[512,768]{1,0:T(8,128)(2,1)S(1)} %bitcast.55, bf16[512,768]{1,0:T(8,128)(2,1)S(1)} %bitcast.58, bf16[768,1536]{1,0:T(8,128)(2,1)S(1)} %pad_maximum_fusion.wi, bf16[1536,768]{1,0:T(8,128)(2,1)S(1)} %pad_maximum_fusion.1.wo), custom_call_target="tpu_custom_call" | custom-call | flops 1000000 | bytes 100000 | tf_op jit(solution)/shard_map/pallas_call | solution.py:53
  42.2 5.2 %collective-permute-done.7 = bf16[128,1536]{1,0:T(8,128)(2,1)S(1)} collective-permute-done((bf16[128,1536]{1,0:T(8,128)(2,1)S(1)}, bf16[128,1536]{1,0:T(8,128)(2,1)S(1)}, u32[]{:S(2)}, u32[]{:S(2)}) %collective-permute-start.7) | collective-permute-done | bytes 393248 | tf_op jit(solution)/shard_map/ppermute | solution.py:25
  47.6 1.3 collective-permute-start.13
  49.1 2.0 %collective-permute-start.14 = (bf16[128,3072]{1,0:T(8,128)(2,1)S(1)}, bf16[128,3072]{1,0:T(8,128)(2,1)S(1)}, u32[]{:S(2)}, u32[]{:S(2)}) collective-permute-start(bf16[128,3072]{1,0:T(8,128)(2,1)S(1)} %pad_maximum_fusion.13), channel_id=1, source_target_pairs={{0,6},{2,0},{4,2},{6,4},{1,7},{3,1},{5,3},{7,5},{8,14},{10,8},{12,... | collective-permute-start | bytes 2359304 | tf_op jit(solution)/shard_map/ppermute | solution.py:25
  51.2 3.2 %collective-permute-start.17 = (bf16[128,1536]{1,0:T(8,128)(2,1)S(1)}, bf16[128,1536]{1,0:T(8,128)(2,1)S(1)}, u32[]{:S(2)}, u32[]{:S(2)}) collective-permute-start(bf16[128,1536]{1,0:T(8,128)(2,1)S(1)} %get-tuple-element.98), channel_id=1, source_target_pairs={{0,6},{2,0},{4,2},{6,4},{1,7},{3,1},{5,3},{7,5},{8,14},{10,8},{12,... | collective-permute-start | bytes 1179656 | tf_op jit(solution)/shard_map/ppermute | solution.py:25
  54.4 14.9 %collective-permute-done.13 = bf16[128,3072]{1,0:T(8,128)(2,1)S(1)} collective-permute-done((bf16[128,3072]{1,0:T(8,128)(2,1)S(1)}, bf16[128,3072]{1,0:T(8,128)(2,1)S(1)}, u32[]{:S(2)}, u32[]{:S(2)}) %collective-permute-start.13) | collective-permute-done | bytes 786464 | tf_op jit(solution)/shard_map/ppermute | solution.py:25
  70.7 5.9 %collective-permute-done.16 = bf16[128,1536]{1,0:T(8,128)(2,1)S(1)} collective-permute-done((bf16[128,1536]{1,0:T(8,128)(2,1)S(1)}, bf16[128,1536]{1,0:T(8,128)(2,1)S(1)}, u32[]{:S(2)}, u32[]{:S(2)}) %collective-permute-start.16) | collective-permute-done | bytes 393248 | tf_op jit(solution)/shard_map/ppermute | solution.py:25
  76.8 3.2 %collective-permute-start.21 = (bf16[128,3072]{1,0:T(8,128)(2,1)S(1)}, bf16[128,3072]{1,0:T(8,128)(2,1)S(1)}, u32[]{:S(2)}, u32[]{:S(2)}) collective-permute-start(bf16[128,3072]{1,0:T(8,128)(2,1)S(1)} %pad_maximum_fusion.16), channel_id=1, source_target_pairs={{0,6},{2,0},{4,2},{6,4},{1,7},{3,1},{5,3},{7,5},{8,14},{10,8},{12,... | collective-permute-start | bytes 2359304 | tf_op jit(solution)/shard_map/ppermute | solution.py:25
  80.5 6.6 %collective-permute-done.15 = bf16[128,3072]{1,0:T(8,128)(2,1)S(1)} collective-permute-done((bf16[128,3072]{1,0:T(8,128)(2,1)S(1)}, bf16[128,3072]{1,0:T(8,128)(2,1)S(1)}, u32[]{:S(2)}, u32[]{:S(2)}) %collective-permute-start.15) | collective-permute-done | bytes 786464 | tf_op jit(solution)/shard_map/ppermute | solution.py:25
  87.8 2.9 %collective-permute-start.18 = (bf16[128,3072]{1,0:T(8,128)(2,1)S(1)}, bf16[128,3072]{1,0:T(8,128)(2,1)S(1)}, u32[]{:S(2)}, u32[]{:S(2)}) collective-permute-start(bf16[128,3072]{1,0:T(8,128)(2,1)S(1)} %pad_maximum_fusion.17), channel_id=1, source_target_pairs={{0,6},{2,0},{4,2},{6,4},{1,7},{3,1},{5,3},{7,5},{8,14},{10,8},{12,... | collective-permute-start | bytes 2359304 | tf_op jit(solution)/shard_map/ppermute | solution.py:25
  90.8 7.2 %collective-permute-done.21 = bf16[128,3072]{1,0:T(8,128)(2,1)S(1)} collective-permute-done((bf16[128,3072]{1,0:T(8,128)(2,1)S(1)}, bf16[128,3072]{1,0:T(8,128)(2,1)S(1)}, u32[]{:S(2)}, u32[]{:S(2)}) %collective-permute-start.21) | collective-permute-done | bytes 786464 | tf_op jit(solution)/shard_map/ppermute | solution.py:25
  98.0 4.1 %collective-permute-done.20 = bf16[128,3072]{1,0:T(8,128)(2,1)S(1)} collective-permute-done((bf16[128,3072]{1,0:T(8,128)(2,1)S(1)}, bf16[128,3072]{1,0:T(8,128)(2,1)S(1)}, u32[]{:S(2)}, u32[]{:S(2)}) %collective-permute-start.20) | collective-permute-done | bytes 786464 | tf_op jit(solution)/shard_map/ppermute | solution.py:25
  103.2 9.3 %collective-permute-done.18 = bf16[128,3072]{1,0:T(8,128)(2,1)S(1)} collective-permute-done((bf16[128,3072]{1,0:T(8,128)(2,1)S(1)}, bf16[128,3072]{1,0:T(8,128)(2,1)S(1)}, u32[]{:S(2)}, u32[]{:S(2)}) %collective-permute-start.18) | collective-permute-done | bytes 786464 | tf_op jit(solution)/shard_map/ppermute | solution.py:25
  112.5 3.8 %collective-permute-done.19 = bf16[128,3072]{1,0:T(8,128)(2,1)S(1)} collective-permute-done((bf16[128,3072]{1,0:T(8,128)(2,1)S(1)}, bf16[128,3072]{1,0:T(8,128)(2,1)S(1)}, u32[]{:S(2)}, u32[]{:S(2)}) %collective-permute-start.19) | collective-permute-done | bytes 786464 | tf_op jit(solution)/shard_map/ppermute | solution.py:25
  116.4 0.9 fusion.48
  117.3 2.0 %collective-permute-start.23 = (bf16[128,1536]{1,0:T(8,128)(2,1)S(1)}, bf16[128,1536]{1,0:T(8,128)(2,1)S(1)}, u32[]{:S(2)}, u32[]{:S(2)}) collective-permute-start(bf16[128,1536]{1,0:T(8,128)(2,1)S(1)} %get-tuple-element.108), channel_id=1, source_target_pairs={{0,2},{2,4},{4,6},{6,0},{1,3},{3,5},{5,7},{7,1},{8,10},{10,12},{12... | collective-permute-start | bytes 1179656 | tf_op jit(solution)/shard_map/ppermute | solution.py:25
  120.1 1.0 pad_maximum_fusion.19
  121.1 4.7 %collective-permute-done.22 = bf16[128,1536]{1,0:T(8,128)(2,1)S(1)} collective-permute-done((bf16[128,1536]{1,0:T(8,128)(2,1)S(1)}, bf16[128,1536]{1,0:T(8,128)(2,1)S(1)}, u32[]{:S(2)}, u32[]{:S(2)}) %collective-permute-start.22) | collective-permute-done | bytes 393248 | tf_op jit(solution)/shard_map/ppermute | solution.py:25
  125.8 1.2 collective-permute-done.23
  127.1 1.6 shard_map.69
  128.8 1.0 slice.308
  130.2 1.0 collective-permute-start.29
  131.2 1.0 collective-permute-start.30
  132.8 1.5 slice_add_fusion.1
  134.3 16.2 %collective-permute-done.29 = bf16[128,3072]{1,0:T(8,128)(2,1)} collective-permute-done((bf16[128,3072]{1,0:T(8,128)(2,1)}, bf16[128,3072]{1,0:T(8,128)(2,1)}, u32[]{:S(2)}, u32[]{:S(2)}) %collective-permute-start.29) | collective-permute-done | bytes 786464 | tf_op jit(solution)/shard_map/ppermute | solution.py:25
  150.5 2.0 %collective-permute-done.30 = bf16[128,3072]{1,0:T(8,128)(2,1)} collective-permute-done((bf16[128,3072]{1,0:T(8,128)(2,1)}, bf16[128,3072]{1,0:T(8,128)(2,1)}, u32[]{:S(2)}, u32[]{:S(2)}) %collective-permute-start.30) | collective-permute-done | bytes 786464 | tf_op jit(solution)/shard_map/ppermute | solution.py:25
  152.4 1.3 fusion.49
  154.1 1.2 fusion.47
  155.2 1.8 collective-permute-start.32
  157.2 2.1 %collective-permute-start.27 = (bf16[4,32,384]{2,1,0:T(8,128)(2,1)S(1)}, bf16[4,32,384]{2,1,0:T(8,128)(2,1)S(1)}, u32[]{:S(2)}, u32[]{:S(2)}) collective-permute-start(bf16[4,32,384]{2,1,0:T(8,128)(2,1)S(1)} %get-tuple-element.126), channel_id=1, source_target_pairs={{0,64},{32,96},{64,0},{96,32},{1,65},{33,97},{65,1},{97,33},{2,66}... | collective-permute-start | bytes 294920 | tf_op jit(solution)/shard_map/ppermute | solution.py:25
  159.2 1.2 collective-permute-start.28
  160.5 3.5 %collective-permute-done.26 = bf16[4,32,384]{2,1,0:T(8,128)(2,1)S(1)} collective-permute-done((bf16[4,32,384]{2,1,0:T(8,128)(2,1)S(1)}, bf16[4,32,384]{2,1,0:T(8,128)(2,1)S(1)}, u32[]{:S(2)}, u32[]{:S(2)}) %collective-permute-start.26) | collective-permute-done | bytes 98336 | tf_op jit(solution)/shard_map/ppermute | solution.py:25
  164.0 0.9 collective-permute-done.28
  164.9 2.0 %collective-permute-done.32 = bf16[128,1536]{1,0:T(8,128)(2,1)S(1)} collective-permute-done((bf16[128,1536]{1,0:T(8,128)(2,1)S(1)}, bf16[128,1536]{1,0:T(8,128)(2,1)S(1)}, u32[]{:S(2)}, u32[]{:S(2)}) %collective-permute-start.32) | collective-permute-done | bytes 393248 | tf_op jit(solution)/shard_map/ppermute | solution.py:25
  167.1 1.6 shard_map.70
  168.9 0.8 copy-done.10
  169.8 1.0 copy-done.7
  170.9 1.0 fusion.18
  172.0 1.0 fusion.3
  173.4 0.8 fusion.24
  174.3 0.8 fusion.1
  175.6 1.0 fusion.21
  176.6 0.8 fusion.27
  178.1 1.6 collective-permute-start.35
  179.7 2.9 %collective-permute-start.36 = (bf16[4,32,384]{2,1,0:T(8,128)(2,1)S(1)}, bf16[4,32,384]{2,1,0:T(8,128)(2,1)S(1)}, u32[]{:S(2)}, u32[]{:S(2)}) collective-permute-start(bf16[4,32,384]{2,1,0:T(8,128)(2,1)S(1)} %get-tuple-element.124), channel_id=1, source_target_pairs={{0,80},{16,64},{32,112},{48,96},{64,16},{80,0},{96,48},{112,32},{1... | collective-permute-start | bytes 294920 | tf_op jit(solution)/shard_map/ppermute | solution.py:216
  182.6 3.6 %collective-permute-start.37 = (bf16[4,32,384]{2,1,0:T(8,128)(2,1)S(1)}, bf16[4,32,384]{2,1,0:T(8,128)(2,1)S(1)}, u32[]{:S(2)}, u32[]{:S(2)}) collective-permute-start(bf16[4,32,384]{2,1,0:T(8,128)(2,1)S(1)} %get-tuple-element.121), channel_id=1, source_target_pairs={{0,112},{16,96},{32,16},{48,0},{64,48},{80,32},{96,80},{112,64},{1... | collective-permute-start | bytes 294920 | tf_op jit(solution)/shard_map/ppermute | solution.py:216
  186.2 1.1 broadcast_select_fusion.1
  187.3 1.6 pad_maximum_fusion.3
  189.0 0.8 broadcast_select_fusion.3
  189.8 1.7 pad_maximum_fusion.2
  (129 shorter events, 15.0 us)
Async XLA Ops:
  1.7 10.4 %collective-permute-start.3 = (bf16[4,32,768]{2,1,0:T(8,128)(2,1)S(1)}, bf16[4,32,768]{2,1,0:T(8,128)(2,1)S(1)}, u32[]{:S(2)}, u32[]{:S(2)}) collective-permute-start(bf16[4,32,768]{2,1,0:T(8,128)(2,1)S(1)} %fusion.31), channel_id=1, source_target_pairs={{0,16},{16,0},{1,17},{17,1},{2,18},{18,2},{3,19},{19,3},{4,20},{20... | collective-permute-start | bytes 589832 | tf_op jit(solution)/shard_map/ppermute | solution.py:25
  4.9 11.1 %collective-permute-start = (bf16[4,32,768]{2,1,0:T(8,128)(2,1)S(1)}, bf16[4,32,768]{2,1,0:T(8,128)(2,1)S(1)}, u32[]{:S(2)}, u32[]{:S(2)}) collective-permute-start(bf16[4,32,768]{2,1,0:T(8,128)(2,1)S(1)} %fusion.31), channel_id=1, source_target_pairs={{0,96},{32,0},{64,32},{96,64},{1,97},{33,1},{65,33},{97,65},{2,98}... | collective-permute-start | bytes 589832 | tf_op jit(solution)/shard_map/ppermute | solution.py:25
  7.9 9.4 %collective-permute-start.1 = (bf16[4,32,768]{2,1,0:T(8,128)(2,1)S(1)}, bf16[4,32,768]{2,1,0:T(8,128)(2,1)S(1)}, u32[]{:S(2)}, u32[]{:S(2)}) collective-permute-start(bf16[4,32,768]{2,1,0:T(8,128)(2,1)S(1)} %fusion.31), channel_id=1, source_target_pairs={{0,64},{32,96},{64,0},{96,32},{1,65},{33,97},{65,1},{97,33},{2,66}... | collective-permute-start | bytes 589832 | tf_op jit(solution)/shard_map/ppermute | solution.py:25
  8.6 11.2 %collective-permute-start.2 = (bf16[4,32,768]{2,1,0:T(8,128)(2,1)S(1)}, bf16[4,32,768]{2,1,0:T(8,128)(2,1)S(1)}, u32[]{:S(2)}, u32[]{:S(2)}) collective-permute-start(bf16[4,32,768]{2,1,0:T(8,128)(2,1)S(1)} %fusion.31), channel_id=1, source_target_pairs={{0,32},{32,64},{64,96},{96,0},{1,33},{33,65},{65,97},{97,1},{2,34}... | collective-permute-start | bytes 589832 | tf_op jit(solution)/shard_map/ppermute | solution.py:25
  9.5 2.4 %copy-start.13 = (bf16[384,3072]{1,0:T(8,128)(2,1)S(1)}, bf16[384,3072]{1,0:T(8,128)(2,1)}, u32[]{:S(2)}) copy-start(bf16[384,3072]{1,0:T(8,128)(2,1)} %param.6) | copy-start | bytes 7077892
  19.8 2.4 %collective-permute-start.4 = (bf16[4,128,768]{2,1,0:T(8,128)(2,1)S(1)}, bf16[4,128,768]{2,1,0:T(8,128)(2,1)S(1)}, u32[]{:S(2)}, u32[]{:S(2)}) collective-permute-start(bf16[4,128,768]{2,1,0:T(8,128)(2,1)S(1)} %constant_dynamic-update-slice_fusion), channel_id=1, source_target_pairs={{0,1},{1,0},{2,3},{3,2},{4,5},{5,4},{6,7},{7,6},{8,9},{9,8},{10,11... | collective-permute-start | bytes 2359304 | tf_op jit(solution)/shard_map/ppermute | solution.py:25
  19.9 4.9 %collective-permute-start.5 = (bf16[384,1536]{1,0:T(8,128)(2,1)S(1)}, bf16[384,1536]{1,0:T(8,128)(2,1)S(1)}, u32[]{:S(2)}, u32[]{:S(2)}) collective-permute-start(bf16[384,1536]{1,0:T(8,128)(2,1)S(1)} %get-tuple-element.92), channel_id=1, source_target_pairs={{0,1},{1,0},{2,3},{3,2},{4,5},{5,4},{6,7},{7,6},{8,9},{9,8},{10,11... | collective-permute-start | bytes 3538952 | tf_op jit(solution)/shard_map/ppermute | solution.py:25
  20.4 5.1 %collective-permute-start.6 = (bf16[1536,384]{1,0:T(8,128)(2,1)S(1)}, bf16[1536,384]{1,0:T(8,128)(2,1)S(1)}, u32[]{:S(2)}, u32[]{:S(2)}) collective-permute-start(bf16[1536,384]{1,0:T(8,128)(2,1)S(1)} %get-tuple-element.90), channel_id=1, source_target_pairs={{0,1},{1,0},{2,3},{3,2},{4,5},{5,4},{6,7},{7,6},{8,9},{9,8},{10,11... | collective-permute-start | bytes 3538952 | tf_op jit(solution)/shard_map/ppermute | solution.py:25
  20.5 9.3 %collective-permute-start.10 = (bf16[4,32,768]{2,1,0:T(8,128)(2,1)S(1)}, bf16[4,32,768]{2,1,0:T(8,128)(2,1)S(1)}, u32[]{:S(2)}, u32[]{:S(2)}) collective-permute-start(bf16[4,32,768]{2,1,0:T(8,128)(2,1)S(1)} %collective-permute-done.3), channel_id=1, source_target_pairs={{0,64},{32,96},{64,0},{96,32},{1,65},{33,97},{65,1},{97,33},{2,66}... | collective-permute-start | bytes 589832 | tf_op jit(solution)/shard_map/ppermute | solution.py:25
  21.1 12.3 %collective-permute-start.11 = (bf16[4,32,768]{2,1,0:T(8,128)(2,1)S(1)}, bf16[4,32,768]{2,1,0:T(8,128)(2,1)S(1)}, u32[]{:S(2)}, u32[]{:S(2)}) collective-permute-start(bf16[4,32,768]{2,1,0:T(8,128)(2,1)S(1)} %collective-permute-done.3), channel_id=1, source_target_pairs={{0,32},{32,64},{64,96},{96,0},{1,33},{33,65},{65,97},{97,1},{2,34}... | collective-permute-start | bytes 589832 | tf_op jit(solution)/shard_map/ppermute | solution.py:25
  22.2 11.3 %collective-permute-start.9 = (bf16[4,32,768]{2,1,0:T(8,128)(2,1)S(1)}, bf16[4,32,768]{2,1,0:T(8,128)(2,1)S(1)}, u32[]{:S(2)}, u32[]{:S(2)}) collective-permute-start(bf16[4,32,768]{2,1,0:T(8,128)(2,1)S(1)} %collective-permute-done.3), channel_id=1, source_target_pairs={{0,96},{32,0},{64,32},{96,64},{1,97},{33,1},{65,33},{97,65},{2,98}... | collective-permute-start | bytes 589832 | tf_op jit(solution)/shard_map/ppermute | solution.py:25
  24.8 1.0 copy-start.6
  33.5 4.4 %collective-permute-start.12 = (bf16[4,128,768]{2,1,0:T(8,128)(2,1)S(1)}, bf16[4,128,768]{2,1,0:T(8,128)(2,1)S(1)}, u32[]{:S(2)}, u32[]{:S(2)}) collective-permute-start(bf16[4,128,768]{2,1,0:T(8,128)(2,1)S(1)} %constant_dynamic-update-slice_fusion.4), channel_id=1, source_target_pairs={{0,1},{1,0},{2,3},{3,2},{4,5},{5,4},{6,7},{7,6},{8,9},{9,8},{10,11... | collective-permute-start | bytes 2359304 | tf_op jit(solution)/shard_map/ppermute | solution.py:25
  33.7 13.8 %collective-permute-start.7 = (bf16[128,1536]{1,0:T(8,128)(2,1)S(1)}, bf16[128,1536]{1,0:T(8,128)(2,1)S(1)}, u32[]{:S(2)}, u32[]{:S(2)}) collective-permute-start(bf16[128,1536]{1,0:T(8,128)(2,1)S(1)} %get-tuple-element.104), channel_id=1, source_target_pairs={{0,2},{2,4},{4,6},{6,0},{1,3},{3,5},{5,7},{7,1},{8,10},{10,12},{12... | collective-permute-start | bytes 1179656 | tf_op jit(solution)/shard_map/ppermute | solution.py:25
  35.6 11.8 %collective-permute-start.8 = (bf16[128,1536]{1,0:T(8,128)(2,1)S(1)}, bf16[128,1536]{1,0:T(8,128)(2,1)S(1)}, u32[]{:S(2)}, u32[]{:S(2)}) collective-permute-start(bf16[128,1536]{1,0:T(8,128)(2,1)S(1)} %get-tuple-element.102), channel_id=1, source_target_pairs={{0,6},{2,0},{4,2},{6,4},{1,7},{3,1},{5,3},{7,5},{8,14},{10,8},{12,... | collective-permute-start | bytes 1179656 | tf_op jit(solution)/shard_map/ppermute | solution.py:25
  38.1 3.6 %copy-start.4 = (bf16[4,128,768]{2,1,0:T(8,128)(2,1)}, bf16[4,128,768]{2,1,0:T(8,128)(2,1)S(1)}, u32[]{:S(2)}) copy-start(bf16[4,128,768]{2,1,0:T(8,128)(2,1)S(1)} %pad_maximum_fusion.11) | copy-start | bytes 2359300
  38.2 3.6 %copy-start.2 = (bf16[4,128,768]{2,1,0:T(8,128)(2,1)}, bf16[4,128,768]{2,1,0:T(8,128)(2,1)S(1)}, u32[]{:S(2)}) copy-start(bf16[4,128,768]{2,1,0:T(8,128)(2,1)S(1)} %pad_maximum_fusion.10) | copy-start | bytes 2359300
  47.6 21.7 %collective-permute-start.13 = (bf16[128,3072]{1,0:T(8,128)(2,1)S(1)}, bf16[128,3072]{1,0:T(8,128)(2,1)S(1)}, u32[]{:S(2)}, u32[]{:S(2)}) collective-permute-start(bf16[128,3072]{1,0:T(8,128)(2,1)S(1)} %pad_maximum_fusion.12), channel_id=1, source_target_pairs={{0,2},{2,4},{4,6},{6,0},{1,3},{3,5},{5,7},{7,1},{8,10},{10,12},{12... | collective-permute-start | bytes 2359304 | tf_op jit(solution)/shard_map/ppermute | solution.py:25
  49.1 20.5 %collective-permute-start.14 = (bf16[128,3072]{1,0:T(8,128)(2,1)S(1)}, bf16[128,3072]{1,0:T(8,128)(2,1)S(1)}, u32[]{:S(2)}, u32[]{:S(2)}) collective-permute-start(bf16[128,3072]{1,0:T(8,128)(2,1)S(1)} %pad_maximum_fusion.13), channel_id=1, source_target_pairs={{0,6},{2,0},{4,2},{6,4},{1,7},{3,1},{5,3},{7,5},{8,14},{10,8},{12,... | collective-permute-start | bytes 2359304 | tf_op jit(solution)/shard_map/ppermute | solution.py:25
  51.1 25.5 %collective-permute-start.16 = (bf16[128,1536]{1,0:T(8,128)(2,1)S(1)}, bf16[128,1536]{1,0:T(8,128)(2,1)S(1)}, u32[]{:S(2)}, u32[]{:S(2)}) collective-permute-start(bf16[128,1536]{1,0:T(8,128)(2,1)S(1)} %get-tuple-element.96), channel_id=1, source_target_pairs={{0,2},{2,4},{4,6},{6,0},{1,3},{3,5},{5,7},{7,1},{8,10},{10,12},{12... | collective-permute-start | bytes 1179656 | tf_op jit(solution)/shard_map/ppermute | solution.py:25
  51.2 25.4 %collective-permute-start.17 = (bf16[128,1536]{1,0:T(8,128)(2,1)S(1)}, bf16[128,1536]{1,0:T(8,128)(2,1)S(1)}, u32[]{:S(2)}, u32[]{:S(2)}) collective-permute-start(bf16[128,1536]{1,0:T(8,128)(2,1)S(1)} %get-tuple-element.98), channel_id=1, source_target_pairs={{0,6},{2,0},{4,2},{6,4},{1,7},{3,1},{5,3},{7,5},{8,14},{10,8},{12,... | collective-permute-start | bytes 1179656 | tf_op jit(solution)/shard_map/ppermute | solution.py:25
  70.1 17.0 %collective-permute-start.15 = (bf16[128,3072]{1,0:T(8,128)(2,1)S(1)}, bf16[128,3072]{1,0:T(8,128)(2,1)S(1)}, u32[]{:S(2)}, u32[]{:S(2)}) collective-permute-start(bf16[128,3072]{1,0:T(8,128)(2,1)S(1)} %pad_maximum_fusion.14), channel_id=1, source_target_pairs={{0,8},{8,0},{1,9},{9,1},{2,10},{10,2},{3,11},{11,3},{4,12},{12,4},... | collective-permute-start | bytes 2359304 | tf_op jit(solution)/shard_map/ppermute | solution.py:25
  76.8 21.2 %collective-permute-start.21 = (bf16[128,3072]{1,0:T(8,128)(2,1)S(1)}, bf16[128,3072]{1,0:T(8,128)(2,1)S(1)}, u32[]{:S(2)}, u32[]{:S(2)}) collective-permute-start(bf16[128,3072]{1,0:T(8,128)(2,1)S(1)} %pad_maximum_fusion.16), channel_id=1, source_target_pairs={{0,6},{2,0},{4,2},{6,4},{1,7},{3,1},{5,3},{7,5},{8,14},{10,8},{12,... | collective-permute-start | bytes 2359304 | tf_op jit(solution)/shard_map/ppermute | solution.py:25
  80.2 21.9 %collective-permute-start.20 = (bf16[128,3072]{1,0:T(8,128)(2,1)S(1)}, bf16[128,3072]{1,0:T(8,128)(2,1)S(1)}, u32[]{:S(2)}, u32[]{:S(2)}) collective-permute-start(bf16[128,3072]{1,0:T(8,128)(2,1)S(1)} %pad_maximum_fusion.15), channel_id=1, source_target_pairs={{0,2},{2,4},{4,6},{6,0},{1,3},{3,5},{5,7},{7,1},{8,10},{10,12},{12... | collective-permute-start | bytes 2359304 | tf_op jit(solution)/shard_map/ppermute | solution.py:25
  87.8 24.6 %collective-permute-start.18 = (bf16[128,3072]{1,0:T(8,128)(2,1)S(1)}, bf16[128,3072]{1,0:T(8,128)(2,1)S(1)}, u32[]{:S(2)}, u32[]{:S(2)}) collective-permute-start(bf16[128,3072]{1,0:T(8,128)(2,1)S(1)} %pad_maximum_fusion.17), channel_id=1, source_target_pairs={{0,6},{2,0},{4,2},{6,4},{1,7},{3,1},{5,3},{7,5},{8,14},{10,8},{12,... | collective-permute-start | bytes 2359304 | tf_op jit(solution)/shard_map/ppermute | solution.py:25
  90.8 25.6 %collective-permute-start.19 = (bf16[128,3072]{1,0:T(8,128)(2,1)S(1)}, bf16[128,3072]{1,0:T(8,128)(2,1)S(1)}, u32[]{:S(2)}, u32[]{:S(2)}) collective-permute-start(bf16[128,3072]{1,0:T(8,128)(2,1)S(1)} %pad_maximum_fusion.17), channel_id=1, source_target_pairs={{0,2},{2,4},{4,6},{6,0},{1,3},{3,5},{5,7},{7,1},{8,10},{10,12},{12... | collective-permute-start | bytes 2359304 | tf_op jit(solution)/shard_map/ppermute | solution.py:25
  102.5 14.8 %collective-permute-start.24 = (bf16[128,3072]{1,0:T(8,128)(2,1)S(1)}, bf16[128,3072]{1,0:T(8,128)(2,1)S(1)}, u32[]{:S(2)}, u32[]{:S(2)}) collective-permute-start(bf16[128,3072]{1,0:T(8,128)(2,1)S(1)} %pad_maximum_fusion.18), channel_id=1, source_target_pairs={{0,8},{8,0},{1,9},{9,1},{2,10},{10,2},{3,11},{11,3},{4,12},{12,4},... | collective-permute-start | bytes 2359304 | tf_op jit(solution)/shard_map/ppermute | solution.py:25
  116.4 3.6 %copy-start.14 = (bf16[128,1536]{1,0:T(8,128)(2,1)}, bf16[128,1536]{1,0:T(8,128)(2,1)S(1)}, u32[]{:S(2)}) copy-start(bf16[128,1536]{1,0:T(8,128)(2,1)S(1)} %get-tuple-element.112) | copy-start | bytes 1179652
  117.3 8.5 %collective-permute-start.22 = (bf16[128,1536]{1,0:T(8,128)(2,1)S(1)}, bf16[128,1536]{1,0:T(8,128)(2,1)S(1)}, u32[]{:S(2)}, u32[]{:S(2)}) collective-permute-start(bf16[128,1536]{1,0:T(8,128)(2,1)S(1)} %get-tuple-element.112), channel_id=1, source_target_pairs={{0,6},{2,0},{4,2},{6,4},{1,7},{3,1},{5,3},{7,5},{8,14},{10,8},{12,... | collective-permute-start | bytes 1179656 | tf_op jit(solution)/shard_map/ppermute | solution.py:25
  117.3 9.7 %collective-permute-start.23 = (bf16[128,1536]{1,0:T(8,128)(2,1)S(1)}, bf16[128,1536]{1,0:T(8,128)(2,1)S(1)}, u32[]{:S(2)}, u32[]{:S(2)}) collective-permute-start(bf16[128,1536]{1,0:T(8,128)(2,1)S(1)} %get-tuple-element.108), channel_id=1, source_target_pairs={{0,2},{2,4},{4,6},{6,0},{1,3},{3,5},{5,7},{7,1},{8,10},{10,12},{12... | collective-permute-start | bytes 1179656 | tf_op jit(solution)/shard_map/ppermute | solution.py:25
  120.0 7.0 %copy-start.9 = (bf16[128,1536]{1,0:T(8,128)(2,1)}, bf16[128,1536]{1,0:T(8,128)(2,1)S(1)}, u32[]{:S(2)}) copy-start(bf16[128,1536]{1,0:T(8,128)(2,1)S(1)} %get-tuple-element.81) | copy-start | bytes 1179652
  120.0 7.0 %copy-start.11 = (bf16[128,1536]{1,0:T(8,128)(2,1)}, bf16[128,1536]{1,0:T(8,128)(2,1)S(1)}, u32[]{:S(2)}) copy-start(bf16[128,1536]{1,0:T(8,128)(2,1)S(1)} %get-tuple-element.82) | copy-start | bytes 1179652
  125.8 1.2 copy-start.17
  127.1 1.7 copy-start
  128.8 1.4 copy-start.8
  130.2 2.6 %collective-permute-start.25 = (f32[512,384]{1,0:T(8,128)}, f32[512,384]{1,0:T(8,128)}, u32[]{:S(2)}, u32[]{:S(2)}) collective-permute-start(f32[512,384]{1,0:T(8,128)} %slice.308), channel_id=1, source_target_pairs={{0,1},{1,0},{2,3},{3,2},{4,5},{5,4},{6,7},{7,6},{8,9},{9,8},{10,11... | collective-permute-start | bytes 2359304 | tf_op jit(solution)/shard_map/ppermute | solution.py:25
  130.2 20.3 %collective-permute-start.29 = (bf16[128,3072]{1,0:T(8,128)(2,1)}, bf16[128,3072]{1,0:T(8,128)(2,1)}, u32[]{:S(2)}, u32[]{:S(2)}) collective-permute-start(bf16[128,3072]{1,0:T(8,128)(2,1)} %pad_maximum_fusion.19), channel_id=1, source_target_pairs={{0,6},{2,0},{4,2},{6,4},{1,7},{3,1},{5,3},{7,5},{8,14},{10,8},{12,... | collective-permute-start | bytes 2359304 | tf_op jit(solution)/shard_map/ppermute | solution.py:25
  131.2 21.2 %collective-permute-start.30 = (bf16[128,3072]{1,0:T(8,128)(2,1)}, bf16[128,3072]{1,0:T(8,128)(2,1)}, u32[]{:S(2)}, u32[]{:S(2)}) collective-permute-start(bf16[128,3072]{1,0:T(8,128)(2,1)} %pad_maximum_fusion.19), channel_id=1, source_target_pairs={{0,2},{2,4},{4,6},{6,0},{1,3},{3,5},{5,7},{7,1},{8,10},{10,12},{12... | collective-permute-start | bytes 2359304 | tf_op jit(solution)/shard_map/ppermute | solution.py:25
  152.4 8.0 %copy-start.15 = (bf16[128,1536]{1,0:T(8,128)(2,1)S(1)}, bf16[128,1536]{1,0:T(8,128)(2,1)}, u32[]{:S(2)}) copy-start(bf16[128,1536]{1,0:T(8,128)(2,1)} %copy-done.14) | copy-start | bytes 1179652
  152.4 8.0 %copy-start.16 = (bf16[128,1536]{1,0:T(8,128)(2,1)S(1)}, bf16[128,1536]{1,0:T(8,128)(2,1)}, u32[]{:S(2)}) copy-start(bf16[128,1536]{1,0:T(8,128)(2,1)} %get-tuple-element.107) | copy-start | bytes 1179652
  152.4 8.0 %copy-start.18 = (bf16[128,1536]{1,0:T(8,128)(2,1)S(1)}, bf16[128,1536]{1,0:T(8,128)(2,1)}, u32[]{:S(2)}) copy-start(bf16[128,1536]{1,0:T(8,128)(2,1)} %copy-done.17) | copy-start | bytes 1179652
  153.7 11.2 %collective-permute-start.31 = (bf16[128,1536]{1,0:T(8,128)(2,1)S(1)}, bf16[128,1536]{1,0:T(8,128)(2,1)S(1)}, u32[]{:S(2)}, u32[]{:S(2)}) collective-permute-start(bf16[128,1536]{1,0:T(8,128)(2,1)S(1)} %get-tuple-element.110), channel_id=1, source_target_pairs={{0,6},{2,0},{4,2},{6,4},{1,7},{3,1},{5,3},{7,5},{8,14},{10,8},{12,... | collective-permute-start | bytes 1179656 | tf_op jit(solution)/shard_map/ppermute | solution.py:25
  155.2 11.7 %collective-permute-start.32 = (bf16[128,1536]{1,0:T(8,128)(2,1)S(1)}, bf16[128,1536]{1,0:T(8,128)(2,1)S(1)}, u32[]{:S(2)}, u32[]{:S(2)}) collective-permute-start(bf16[128,1536]{1,0:T(8,128)(2,1)S(1)} %get-tuple-element.106), channel_id=1, source_target_pairs={{0,2},{2,4},{4,6},{6,0},{1,3},{3,5},{5,7},{7,1},{8,10},{10,12},{12... | collective-permute-start | bytes 1179656 | tf_op jit(solution)/shard_map/ppermute | solution.py:25
  157.1 6.9 %collective-permute-start.26 = (bf16[4,32,384]{2,1,0:T(8,128)(2,1)S(1)}, bf16[4,32,384]{2,1,0:T(8,128)(2,1)S(1)}, u32[]{:S(2)}, u32[]{:S(2)}) collective-permute-start(bf16[4,32,384]{2,1,0:T(8,128)(2,1)S(1)} %get-tuple-element.127), channel_id=1, source_target_pairs={{0,32},{32,64},{64,96},{96,0},{1,33},{33,65},{65,97},{97,1},{2,34}... | collective-permute-start | bytes 294920 | tf_op jit(solution)/shard_map/ppermute | solution.py:25
  157.2 6.9 %collective-permute-start.27 = (bf16[4,32,384]{2,1,0:T(8,128)(2,1)S(1)}, bf16[4,32,384]{2,1,0:T(8,128)(2,1)S(1)}, u32[]{:S(2)}, u32[]{:S(2)}) collective-permute-start(bf16[4,32,384]{2,1,0:T(8,128)(2,1)S(1)} %get-tuple-element.126), channel_id=1, source_target_pairs={{0,64},{32,96},{64,0},{96,32},{1,65},{33,97},{65,1},{97,33},{2,66}... | collective-permute-start | bytes 294920 | tf_op jit(solution)/shard_map/ppermute | solution.py:25
  159.2 5.7 %collective-permute-start.28 = (bf16[4,32,384]{2,1,0:T(8,128)(2,1)S(1)}, bf16[4,32,384]{2,1,0:T(8,128)(2,1)S(1)}, u32[]{:S(2)}, u32[]{:S(2)}) collective-permute-start(bf16[4,32,384]{2,1,0:T(8,128)(2,1)S(1)} %get-tuple-element.125), channel_id=1, source_target_pairs={{0,96},{32,0},{64,32},{96,64},{1,97},{33,1},{65,33},{97,65},{2,98}... | collective-permute-start | bytes 294920 | tf_op jit(solution)/shard_map/ppermute | solution.py:25
  160.4 6.6 %copy-start.12 = (bf16[128,1536]{1,0:T(8,128)(2,1)S(1)}, bf16[128,1536]{1,0:T(8,128)(2,1)}, u32[]{:S(2)}) copy-start(bf16[128,1536]{1,0:T(8,128)(2,1)} %copy-done.11) | copy-start | bytes 1179652
  168.7 1.0 copy-start.10
  168.8 8.6 %collective-permute-start.33 = (f32[512,384]{1,0:T(8,128)S(1)}, f32[512,384]{1,0:T(8,128)S(1)}, u32[]{:S(2)}, u32[]{:S(2)}) collective-permute-start(f32[512,384]{1,0:T(8,128)S(1)} %slice.314), channel_id=1, source_target_pairs={{0,1},{1,0},{2,3},{3,2},{4,5},{5,4},{6,7},{7,6},{8,9},{9,8},{10,11... | collective-permute-start | bytes 2359304 | tf_op jit(solution)/shard_map/ppermute | solution.py:25
  169.7 1.1 copy-start.7
  170.9 1.1 copy-start.5
  172.0 1.4 copy-start.1
  173.0 1.2 copy-start.3
  173.0 9.5 %collective-permute-start.39 = (bf16[1536,384]{1,0:T(8,128)(2,1)S(1)}, bf16[1536,384]{1,0:T(8,128)(2,1)S(1)}, u32[]{:S(2)}, u32[]{:S(2)}) collective-permute-start(bf16[1536,384]{1,0:T(8,128)(2,1)S(1)} %fusion.3), channel_id=1, source_target_pairs={{0,1},{1,0},{2,3},{3,2},{4,5},{5,4},{6,7},{7,6},{8,9},{9,8},{10,11... | collective-permute-start | bytes 3538952 | tf_op jit(solution)/shard_map/ppermute | solution.py:25
  175.1 13.9 %collective-permute-start.38 = (bf16[384,1536]{1,0:T(8,128)(2,1)S(1)}, bf16[384,1536]{1,0:T(8,128)(2,1)S(1)}, u32[]{:S(2)}, u32[]{:S(2)}) collective-permute-start(bf16[384,1536]{1,0:T(8,128)(2,1)S(1)} %fusion.1), channel_id=1, source_target_pairs={{0,1},{1,0},{2,3},{3,2},{4,5},{5,4},{6,7},{7,6},{8,9},{9,8},{10,11... | collective-permute-start | bytes 3538952 | tf_op jit(solution)/shard_map/ppermute | solution.py:25
  177.5 14.0 %collective-permute-start.34 = (bf16[4,32,384]{2,1,0:T(8,128)(2,1)S(1)}, bf16[4,32,384]{2,1,0:T(8,128)(2,1)S(1)}, u32[]{:S(2)}, u32[]{:S(2)}) collective-permute-start(bf16[4,32,384]{2,1,0:T(8,128)(2,1)S(1)} %get-tuple-element.123), channel_id=1, source_target_pairs={{0,16},{16,0},{32,48},{48,32},{64,80},{80,64},{96,112},{112,96},{1... | collective-permute-start | bytes 294920 | tf_op jit(solution)/shard_map/ppermute | solution.py:216
  178.1 13.4 %collective-permute-start.35 = (bf16[4,32,384]{2,1,0:T(8,128)(2,1)S(1)}, bf16[4,32,384]{2,1,0:T(8,128)(2,1)S(1)}, u32[]{:S(2)}, u32[]{:S(2)}) collective-permute-start(bf16[4,32,384]{2,1,0:T(8,128)(2,1)S(1)} %get-tuple-element.122), channel_id=1, source_target_pairs={{0,48},{16,32},{32,80},{48,64},{64,112},{80,96},{96,16},{112,0},{1... | collective-permute-start | bytes 294920 | tf_op jit(solution)/shard_map/ppermute | solution.py:216
  179.7 11.8 %collective-permute-start.36 = (bf16[4,32,384]{2,1,0:T(8,128)(2,1)S(1)}, bf16[4,32,384]{2,1,0:T(8,128)(2,1)S(1)}, u32[]{:S(2)}, u32[]{:S(2)}) collective-permute-start(bf16[4,32,384]{2,1,0:T(8,128)(2,1)S(1)} %get-tuple-element.124), channel_id=1, source_target_pairs={{0,80},{16,64},{32,112},{48,96},{64,16},{80,0},{96,48},{112,32},{1... | collective-permute-start | bytes 294920 | tf_op jit(solution)/shard_map/ppermute | solution.py:216
  182.6 9.0 %collective-permute-start.37 = (bf16[4,32,384]{2,1,0:T(8,128)(2,1)S(1)}, bf16[4,32,384]{2,1,0:T(8,128)(2,1)S(1)}, u32[]{:S(2)}, u32[]{:S(2)}) collective-permute-start(bf16[4,32,384]{2,1,0:T(8,128)(2,1)S(1)} %get-tuple-element.121), channel_id=1, source_target_pairs={{0,112},{16,96},{32,16},{48,0},{64,48},{80,32},{96,80},{112,64},{1... | collective-permute-start | bytes 294920 | tf_op jit(solution)/shard_map/ppermute | solution.py:216
